TPU v7x, 512 devices: a whole 4x4x16 slice. The times are simulated.
512 devices in a mesh: seq: 64 (over x_lo, z, core), chan: 8 (over y, x_hi).
Axes of the slice: x: 4 (x_hi: 2, x_lo: 2; x = x_hi * 2 + x_lo), y: 4, z: 16, core: 2. Of those that a mesh axis runs over, the one named last changes fastest.
Arguments:
- query_proj: bfloat16 [8192, 4096], P('seq', 'chan'), may hold values from -6 to 6
- key_proj: bfloat16 [8192, 4096], P('seq', 'chan'), may hold values from -6 to 6
- value_proj: bfloat16 [8192, 4096], P('seq', 'chan'), may hold values from -6 to 6
- filter_taps: float32 [8192, 4096], P('seq', 'chan'), may hold values from -6 to 6
- skip_bias: float32 [4096], P('chan'), may hold values from -3 to 3
- out_weight: bfloat16 [4096, 4096], P('seq', 'chan'), may hold values from -0.09375 to 0.09375
Outputs:
- operator_out: bfloat16 [8192, 4096], P('seq', 'chan')
- convolved: float32 [8192, 4096], P('seq', 'chan')
All inputs are finite; a program needn't handle non-finite values.
Results may differ from a plain program's by a relative error of at most 0.0049.
Values may be sent and summed in bfloat16 or wider, within the bound.
A program may use at most 64 MiB of HBM per device.

v0:
```python
import math

import jax
import jax.numpy as jnp
from jax import lax
from jax.sharding import PartitionSpec as P

PRECISE = lax.Precision.HIGHEST


def regroup(stacked):
    return lax.all_to_all(stacked, "seq", split_axis=0, concat_axis=1, tiled=True)


def along_time(table, values):
    return jnp.einsum("kt,jmtc->jmkc", table, values, precision=PRECISE)


def along_freq(table, values):
    return jnp.einsum("kt,jtc->jkc", table, values, precision=PRECISE)


def body(query_proj, key_proj, value_proj, filter_taps, skip_bias, out_weight):
    tok_rows, slab_width = query_proj.shape
    shards = lax.axis_size("seq")
    my_index = lax.axis_index("seq")
    lane_count = tok_rows // shards
    flat_size = lane_count * slab_width
    fft_length = 2 * tok_rows * shards
    signal = key_proj.astype(jnp.float32) * value_proj.astype(jnp.float32)
    stacked = jnp.stack(
        [signal.reshape(shards, flat_size), filter_taps.reshape(shards, flat_size)], axis=1
    )
    arrived = regroup(stacked).reshape(shards, 2, flat_size)
    pair_index = jnp.arange(shards, dtype=jnp.int32)
    freq_rows = jnp.stack([pair_index, 2 * shards - 1 - pair_index], axis=1).reshape(2 * shards)
    block_cols = jnp.arange(shards, dtype=jnp.int32)
    first_phase = freq_rows[:, None] * block_cols[None, :] % (2 * shards)
    first_angle = first_phase.astype(jnp.float32) * (-2.0 * math.pi / (2 * shards))
    first_cos = jnp.cos(first_angle)
    first_sin = jnp.sin(first_angle)
    cos_part = jnp.einsum("kp,pmf->kmf", first_cos, arrived, precision=PRECISE)
    sin_part = jnp.einsum("kp,pmf->kmf", first_sin, arrived, precision=PRECISE)
    first_re = cos_part
    first_im = sin_part
    member_count = first_re.shape[1]
    first_re = first_re.reshape(2 * shards, member_count, lane_count, slab_width)
    first_im = first_im.reshape(2 * shards, member_count, lane_count, slab_width)
    offsets = my_index * lane_count + jnp.arange(lane_count, dtype=jnp.int32)
    twist_phase = freq_rows[:, None] * offsets[None, :] % fft_length
    twist_angle = twist_phase.astype(jnp.float32) * (-2.0 * math.pi / fft_length)
    twist_cos = jnp.cos(twist_angle)
    twist_sin = jnp.sin(twist_angle)
    wide_cos = twist_cos[:, None, :, None]
    wide_sin = twist_sin[:, None, :, None]
    turned_re = first_re * wide_cos - first_im * wide_sin
    turned_im = first_re * wide_sin + first_im * wide_cos
    turned = jnp.stack([turned_re, turned_im], axis=2).reshape(
        2 * shards, member_count * 2, 1, flat_size
    )
    spread = lax.all_to_all(turned, "seq", split_axis=0, concat_axis=2, tiled=True)
    spread = spread.reshape(2, member_count, 2, tok_rows, slab_width)
    time_index = jnp.arange(tok_rows, dtype=jnp.int32)
    second_phase = time_index[:, None] * time_index[None, :] % tok_rows
    second_angle = second_phase.astype(jnp.float32) * (-2.0 * math.pi / tok_rows)
    second_cos = jnp.cos(second_angle)
    second_sin = jnp.sin(second_angle)
    spread_re = spread[:, :, 0]
    spread_im = spread[:, :, 1]
    trans_re = along_time(second_cos, spread_re) - along_time(second_sin, spread_im)
    trans_im = along_time(second_cos, spread_im) + along_time(second_sin, spread_re)
    signal_re = trans_re[:, 0]
    signal_im = trans_im[:, 0]
    kernel_re = trans_re[:, 1]
    kernel_im = trans_im[:, 1]
    product_re = signal_re * kernel_re - signal_im * kernel_im
    product_im = signal_re * kernel_im + signal_im * kernel_re
    back_re = along_freq(second_cos, product_re) + along_freq(second_sin, product_im)
    back_im = along_freq(second_cos, product_im) - along_freq(second_sin, product_re)
    back = jnp.stack([back_re, back_im], axis=1).reshape(2, 2, shards, flat_size)
    returned = lax.all_to_all(back, "seq", split_axis=2, concat_axis=0, tiled=True)
    returned = returned.reshape(2 * shards, 2, lane_count, slab_width)
    ret_re = returned[:, 0]
    ret_im = returned[:, 1]
    narrow_cos = twist_cos[:, :, None]
    narrow_sin = twist_sin[:, :, None]
    untwist_re = (ret_re * narrow_cos + ret_im * narrow_sin).reshape(2 * shards, flat_size)
    untwist_im = (ret_im * narrow_cos - ret_re * narrow_sin).reshape(2 * shards, flat_size)
    convolved = jnp.einsum("kp,kf->pf", first_cos, untwist_re, precision=PRECISE)
    convolved = convolved + jnp.einsum("kp,kf->pf", first_sin, untwist_im, precision=PRECISE)
    convolved = convolved * (1.0 / fft_length)
    convolved = regroup(convolved.reshape(shards, 1, flat_size)).reshape(tok_rows, slab_width)
    mixed_sum = convolved + skip_bias[None, :] * signal
    gated = (query_proj.astype(jnp.float32) * mixed_sum).astype(jnp.bfloat16)
    whole = lax.all_gather(gated, "chan", axis=1, tiled=True)
    result = jnp.dot(
        whole,
        lax.all_gather(out_weight, "seq", axis=0, tiled=True),
        preferred_element_type=jnp.float32,
    )
    return (result.astype(jnp.bfloat16), convolved)


def solution(mesh):
    return jax.shard_map(
        body,
        mesh=mesh,
        in_specs=(
            P("seq", "chan"),
            P("seq", "chan"),
            P("seq", "chan"),
            P("seq", "chan"),
            P("chan"),
            P("seq", "chan"),
        ),
        out_specs=(P("seq", "chan"), P("seq", "chan")),
        check_vma=False,
    )
```

profile of v0, /device:TPU:1, one launch (start us, length us, event | category | flops | bytes accessed | tf_op | source)
XLA Modules:
  0.0 362.6 jit_solution(17964542226756989471)
XLA Ops:
  7.2 1.0 convert_multiply_fusion
  8.2 0.3 stack_reshape.6
  8.5 1.3 stack_reshape.7
  9.7 1.3 pad_maximum_fusion.2
  11.0 18.1 %all-to-all-start = ((f32[64,2,1024]{2,1,0:T(2,128)}), f32[64,2,1024]{2,1,0:T(2,128)S(1)}, u32[]{:S(2)}, u32[]{:S(2)}) async-start(f32[64,2,1024]{2,1,0:T(2,128)} %pad_maximum_fusion.2), calls=%async_computation | async-start | bytes 1048576 | tf_op jit(solution)/shard_map/all_to_all | solution.py:12
  29.2 0.1 mul.246
  29.4 0.1 fusion.67
  29.5 31.3 %all-to-all-done = f32[64,2,1024]{2,1,0:T(2,128)S(1)} async-done(((f32[64,2,1024]{2,1,0:T(2,128)}), f32[64,2,1024]{2,1,0:T(2,128)S(1)}, u32[]{:S(2)}, u32[]{:S(2)}) %all-to-all-start) | async-done | bytes 524320 | tf_op jit(solution)/shard_map/all_to_all | solution.py:12
  60.8 0.6 reshape.223
  61.4 1.2 fusion.21
  62.6 1.4 subtract_bitcast_fusion
  64.0 0.2 pad_maximum_fusion
  64.2 1.8 copy.37
  66.0 3.2 copy.38
  69.2 5.8 %all-to-all-start.1 = ((f32[128,4,1,1024]{3,1,2,0:T(4,128)}), f32[128,4,1,1024]{3,1,2,0:T(4,128)S(1)}, u32[]{:S(2)}, u32[]{:S(2)}) async-start(f32[128,4,1,1024]{3,1,2,0:T(4,128)} %copy.38), calls=%async_computation.1 | async-start | bytes 4194304 | tf_op jit(solution)/shard_map/all_to_all | solution.py:61
  75.1 0.7 all-gather.5.cloned.1.call-update
  75.8 104.6 %all-to-all-done.1 = f32[128,4,1,1024]{3,1,2,0:T(4,128)S(1)} async-done(((f32[128,4,1,1024]{3,1,2,0:T(4,128)}), f32[128,4,1,1024]{3,1,2,0:T(4,128)S(1)}, u32[]{:S(2)}, u32[]{:S(2)}) %all-to-all-start.1) | async-done | bytes 2097184 | tf_op jit(solution)/shard_map/all_to_all | solution.py:61
  180.3 2.6 copy.39
  182.9 1.9 reshape.213
  184.8 1.9 fusion.6
  186.8 1.9 fusion.7
  188.7 1.9 fusion.1
  190.6 1.9 fusion
  192.6 0.1 multiply_subtract_fusion
  192.7 0.8 fusion.12
  193.5 0.8 fusion.3
  194.3 0.2 copy.42
  194.5 0.2 stack.31
  194.7 0.8 fusion.8
  195.5 0.8 fusion.2
  196.4 0.2 copy.43
  196.6 0.2 stack.32
  196.9 2.0 copy.44
  198.9 11.2 %all-to-all-start.2 = ((f32[2,2,64,1024]{3,0,1,2:T(2,128)}), f32[2,2,64,1024]{3,0,1,2:T(2,128)S(1)}, u32[]{:S(2)}, u32[]{:S(2)}) async-start(f32[2,2,64,1024]{3,0,1,2:T(2,128)} %copy.44), calls=%async_computation.2 | async-start | bytes 2097152 | tf_op jit(solution)/shard_map/all_to_all | solution.py:81
  210.4 0.2 mul.274
  210.7 0.2 mul.277
  211.0 53.2 %all-to-all-done.2 = f32[2,2,64,1024]{3,0,1,2:T(2,128)S(1)} async-done(((f32[2,2,64,1024]{3,0,1,2:T(2,128)}), f32[2,2,64,1024]{3,0,1,2:T(2,128)S(1)}, u32[]{:S(2)}, u32[]{:S(2)}) %all-to-all-start.2) | async-done | bytes 1048608 | tf_op jit(solution)/shard_map/all_to_all | solution.py:81
  264.2 0.5 copy.45
  264.7 1.3 reshape.214
  266.0 0.4 fusion.116
  266.6 0.6 fusion.17
  267.2 0.6 fusion.5
  267.8 0.3 copy.48
  268.1 30.5 %all_to_all.48 = f32[64,1,1024]{2,1,0:T(1,128)S(1)} all-to-all(f32[64,1,1024]{2,1,0:T(1,128)S(1)} %copy.48), channel_id=1, replica_groups=mesh['seq'=64,'chan'=8] {'seq'}, dimensions={0} | all-to-all | bytes 524288 | tf_op jit(solution)/shard_map/all_to_all | solution.py:12
  298.6 0.6 reduce
  299.3 0.7 multiply_convert_fusion
  300.1 51.7 %all-gather.3.cloned.1.call-done = bf16[128,4096]{1,0:T(8,128)(2,1)} async-done(((bf16[128,512]{1,0:T(8,128)(2,1)}), bf16[128,4096]{1,0:T(8,128)(2,1)}) %all-gather.3.cloned.1.call-update) | async-done | bytes 1048592 | tf_op jit(solution)/shard_map/all_gather | solution.py:95
  351.9 3.9 %convolution_convert_fusion = bf16[128,512]{1,0:T(8,128)(2,1)} fusion(bf16[128,4096]{1,0:T(8,128)(2,1)} %all-gather.3.cloned.1.call-done, bf16[4096,512]{1,0:T(8,128)(2,1)} %all-gather.5.cloned.1.call-done), kind=kOutput, calls=%fused_computation.12 | convolution fusion | flops 536936448 | bytes 5373952 | tf_op jit(solution)/shard_map/dot_general | solution.py:96
  (27 shorter events, 1.0 us)
Async XLA Ops:
  11.0 49.8 %all-to-all-start = ((f32[64,2,1024]{2,1,0:T(2,128)}), f32[64,2,1024]{2,1,0:T(2,128)S(1)}, u32[]{:S(2)}, u32[]{:S(2)}) async-start(f32[64,2,1024]{2,1,0:T(2,128)} %pad_maximum_fusion.2), calls=%async_computation | async-start | bytes 1048576 | tf_op jit(solution)/shard_map/all_to_all | solution.py:12
  69.2 111.2 %all-to-all-start.1 = ((f32[128,4,1,1024]{3,1,2,0:T(4,128)}), f32[128,4,1,1024]{3,1,2,0:T(4,128)S(1)}, u32[]{:S(2)}, u32[]{:S(2)}) async-start(f32[128,4,1,1024]{3,1,2,0:T(4,128)} %copy.38), calls=%async_computation.1 | async-start | bytes 4194304 | tf_op jit(solution)/shard_map/all_to_all | solution.py:61
  75.0 225.1 %all-gather.5.cloned.1.call-start = ((), (), s32[]{:S(2)}) async-start(), calls=%async_computation.5 | async-start | bytes 4259840 | tf_op jit(solution)/shard_map/all_gather | solution.py:98
  198.9 65.3 %all-to-all-start.2 = ((f32[2,2,64,1024]{3,0,1,2:T(2,128)}), f32[2,2,64,1024]{3,0,1,2:T(2,128)S(1)}, u32[]{:S(2)}, u32[]{:S(2)}) async-start(f32[2,2,64,1024]{3,0,1,2:T(2,128)} %copy.44), calls=%async_computation.2 | async-start | bytes 2097152 | tf_op jit(solution)/shard_map/all_to_all | solution.py:81
  210.1 141.7 %all-gather.3.cloned.1.call-start = ((), (), s32[]{:S(2)}) async-start(), calls=%async_computation.4 | async-start | bytes 1179648 | tf_op jit(solution)/shard_map/all_gather | solution.py:95
  267.2 32.1 %copy-start.1 = (bf16[128,512]{1,0:T(8,128)(2,1)S(1)}, bf16[128,512]{1,0:T(8,128)(2,1)}, u32[]{:S(2)}) copy-start(bf16[128,512]{1,0:T(8,128)(2,1)} %param.8) | copy-start | bytes 393220
  267.2 32.1 %copy-start.2 = (bf16[128,512]{1,0:T(8,128)(2,1)S(1)}, bf16[128,512]{1,0:T(8,128)(2,1)}, u32[]{:S(2)}) copy-start(bf16[128,512]{1,0:T(8,128)(2,1)} %param.7) | copy-start | bytes 393220
  267.2 32.1 %copy-start.3 = (bf16[128,512]{1,0:T(8,128)(2,1)S(1)}, bf16[128,512]{1,0:T(8,128)(2,1)}, u32[]{:S(2)}) copy-start(bf16[128,512]{1,0:T(8,128)(2,1)} %param.6) | copy-start | bytes 393220
  267.2 32.1 %copy-start.4 = (f32[512]{0:T(512)S(1)}, f32[512]{0:T(512)}, u32[]{:S(2)}) copy-start(f32[512]{0:T(512)} %param.10) | copy-start | bytes 6148
  299.3 56.4 %copy-start = (f32[128,512]{1,0:T(8,128)}, f32[128,512]{1,0:T(8,128)S(1)}, u32[]{:S(2)}) copy-start(f32[128,512]{1,0:T(8,128)S(1)} %reshape.216) | copy-start | bytes 786436
Sparse Core Ops, SparseCore 0:
  78.0 165.8 all-gather.4
  300.2 51.6 all-gather.2
where the time goes:
time: 363 us
  waiting for transfers between devices  241 us (66%)
  starting transfers between devices  35.2 us (10%)
  blocking collectives  30.5 us (8%)
  matrix products  18.6 us (5%)
  local copies, waits for them, and re-layouts  18.2 us (5%)
  between operations  14.4 us (4%)
  other arithmetic  4.15 us (1%)
    all_to_all x1, waiting for transfers between devices, body(): lax.all_to_all(turned, 'seq', split_axis=0, concat_axis=2, tiled=True)  105 us
    all_to_all x1, waiting for transfers between devices, body(): lax.all_to_all(back, 'seq', split_axis=2, concat_axis=0, tiled=True)  53.2 us
    all_gather x1, waiting for transfers between devices, body(): whole = lax.all_gather(gated, 'chan', axis=1, tiled=True)  51.7 us
    all_to_all x1, waiting for transfers between devices, regroup(): lax.all_to_all(stacked, 'seq', split_axis=0, concat_axis=1, tiled=True)  31.3 us
    all_to_all x1, blocking collectives, regroup(): lax.all_to_all(stacked, 'seq', split_axis=0, concat_axis=1, tiled=True)  30.5 us
    all_to_all x1, starting transfers between devices, regroup(): lax.all_to_all(stacked, 'seq', split_axis=0, concat_axis=1, tiled=True)  18.1 us
    all_to_all x1, starting transfers between devices, body(): lax.all_to_all(back, 'seq', split_axis=2, concat_axis=0, tiled=True)  11.2 us
    dot_general x4, matrix products, along_time(): return jnp.einsum('kt,jmtc->jmkc', table, values, precision=PRECISE)  7.71 us
  transfers between devices with their start and end apart: 5, of which 4 were waited for; matrix products, arithmetic and copies ran while one was open for 7% of the time, Pallas kernels for 0%

commit v1 on v0

v1 whole, which is shorter than its diff:
```python
import math

import jax
import jax.numpy as jnp
import numpy as np
from jax import lax
from jax.sharding import PartitionSpec as P

PRECISE = lax.Precision.HIGHEST


def tables(blocks, width):
    length = 2 * blocks * width
    half = np.arange(blocks) + 0.5
    angle = 2.0 * math.pi / (2 * blocks) * np.outer(half, np.arange(blocks))
    first = np.concatenate([np.cos(angle), -np.sin(angle)], axis=0)
    last = np.concatenate([np.cos(angle), -np.sin(angle)], axis=0).T * (2.0 / length)
    twist = 2.0 * math.pi / length * np.outer(half, np.arange(width))
    second = 2.0 * math.pi / width * (np.outer(np.arange(width), np.arange(width)) % width)
    c, s = np.cos(second), np.sin(second)
    forward = np.block([[c, -s], [s, c]])
    backward = np.block([[c, s], [-s, c]])
    f32 = lambda a: a.astype(np.float32)
    return f32(first), f32(last), f32(np.cos(twist)), f32(np.sin(twist)), f32(forward), f32(backward)


def body(query_proj, key_proj, value_proj, filter_taps, skip_bias, out_weight):
    tok_rows, slab_width = query_proj.shape
    shards = lax.axis_size("seq")
    own = slab_width // shards
    first, last, tw_cos, tw_sin, forward, backward = tables(shards, tok_rows)
    signal = key_proj.astype(jnp.float32) * value_proj.astype(jnp.float32)
    outgoing = jnp.concatenate(
        [
            signal.astype(jnp.bfloat16).T.reshape(shards, own, tok_rows),
            filter_taps.astype(jnp.bfloat16).T.reshape(shards, own, tok_rows),
        ],
        axis=1,
    )
    arrived = lax.all_to_all(outgoing, "seq", split_axis=0, concat_axis=0, tiled=True)
    arrived = arrived.astype(jnp.float32)
    mixed = jnp.einsum("ka,acb->kcb", first, arrived, precision=PRECISE)
    re, im = mixed[:shards], mixed[shards:]
    wc, ws = tw_cos[:, None, :], tw_sin[:, None, :]
    turned = jnp.concatenate([re * wc + im * ws, im * wc - re * ws], axis=-1)
    freq = jnp.einsum("kcb,bf->kcf", turned, forward, precision=PRECISE)
    fr, fi = freq[..., :tok_rows], freq[..., tok_rows:]
    sr, si, hr, hi = fr[:, :own], fi[:, :own], fr[:, own:], fi[:, own:]
    prod = jnp.concatenate([sr * hr - si * hi, sr * hi + si * hr], axis=-1)
    back = jnp.einsum("kcf,fb->kcb", prod, backward, precision=PRECISE)
    br, bi = back[..., :tok_rows], back[..., tok_rows:]
    unturned = jnp.concatenate([br * wc - bi * ws, bi * wc + br * ws], axis=0)
    conv = jnp.einsum("ak,kcb->acb", last, unturned, precision=PRECISE)
    home = lax.all_to_all(conv.astype(jnp.bfloat16), "seq", split_axis=0, concat_axis=0, tiled=True)
    convolved = home.reshape(slab_width, tok_rows).T.astype(jnp.float32)
    mixed_sum = convolved + skip_bias[None, :] * signal
    gated = (query_proj.astype(jnp.float32) * mixed_sum).astype(jnp.bfloat16)
    whole = lax.all_gather(gated, "chan", axis=1, tiled=True)
    result = jnp.dot(
        whole,
        lax.all_gather(out_weight, "seq", axis=0, tiled=True),
        preferred_element_type=jnp.float32,
    )
    return (result.astype(jnp.bfloat16), convolved)


def solution(mesh):
    return jax.shard_map(
        body,
        mesh=mesh,
        in_specs=(
            P("seq", "chan"),
            P("seq", "chan"),
            P("seq", "chan"),
            P("seq", "chan"),
            P("chan"),
            P("seq", "chan"),
        ),
        out_specs=(P("seq", "chan"), P("seq", "chan")),
        check_vma=False,
    )
```

time: 363 us -> 269 us (0.74)
  waiting for transfers between devices: 241 us -> 195 us
  starting transfers between devices: 35.2 us -> 4.27 us
  local copies, waits for them, and re-layouts: 18.2 us -> 4.91 us
  matrix products: 18.6 us -> 7.83 us
  blocking collectives: 30.5 us -> 40.1 us
    all_to_all x3 -> x1, waiting for transfers between devices: 189 us -> 16.8 us  [body(): lax.all_to_all(conv.astype(jnp.bfloat16), 'seq', split_axis=0, concat_axi...]
    all_gather x1, waiting for transfers between devices: 0.02 us -> 127 us  [body(): lax.all_gather(out_weight, 'seq', axis=0, tiled=True)]
    all_to_all x3 -> x1, starting transfers between devices: 35.2 us -> 4.19 us  [body(): lax.all_to_all(conv.astype(jnp.bfloat16), 'seq', split_axis=0, concat_axi...]
    dot_general x12 -> x4, matrix products: 14.7 us -> 3.91 us  [the longest x1 1.49 us: body(): freq = jnp.einsum('kcb,bf->kcf', turned, forward, precision=PRECISE)]
    all_to_all x1, blocking collectives: 30.5 us -> 40.1 us  [body(): lax.all_to_all(outgoing, 'seq', split_axis=0, concat_axis=0, tiled=True)]
    reshape x5 -> x0, local copies, waits for them, and re-layouts: 6.65 us -> none  [the longest x1 3.16 us: body(): jnp.stack([turned_re, turned_im], axis=2)]
    another operation x7 -> x0, local copies, waits for them, and re-layouts: 5.84 us -> none  [the longest x3 2.35 us: body(): jnp.stack([back_re, back_im], axis=1).reshape(2, 2, shards, flat_size)]
    unnamed x14 -> x19, local copies, waits for them, and re-layouts: 0.42 us -> 4.16 us
  transfers between devices with their start and end apart: 5 -> 3, of which waited for: 4 -> 3; matrix products, arithmetic and copies ran while one was open for 7% -> 0% of each run, Pallas kernels for 0% -> 0%
where the time goes in v1:
time: 269 us
  waiting for transfers between devices  195 us (72%)
  blocking collectives  40.1 us (15%)
  between operations  14.3 us (5%)
  matrix products  7.83 us (3%)
  local copies, waits for them, and re-layouts  4.91 us (2%)
  starting transfers between devices  4.27 us (2%)
    all_gather x1, waiting for transfers between devices, body(): lax.all_gather(out_weight, 'seq', axis=0, tiled=True)  127 us
    all_gather x1, waiting for transfers between devices, body(): whole = lax.all_gather(gated, 'chan', axis=1, tiled=True)  50.2 us
    all_to_all x1, blocking collectives, body(): lax.all_to_all(outgoing, 'seq', split_axis=0, concat_axis=0, tiled=True)  40.1 us
    all_to_all x1, waiting for transfers between devices, body(): lax.all_to_all(conv.astype(jnp.bfloat16), 'seq', split_axis=0, concat_axi...  16.8 us
  transfers between devices with their start and end apart: 3, of which 3 were waited for; matrix products, arithmetic and copies ran while one was open for 0% of the time, Pallas kernels for 0%

profile of v1, /device:TPU:1, one launch (start us, length us, event | category | flops | bytes accessed | tf_op | source)
XLA Modules:
  0.0 268.7 jit_solution(3687249210030016737)
XLA Ops:
  7.2 0.0 copy-start.1
  7.2 1.1 copy.27
  8.2 1.0 copy.28
  9.3 1.1 copy.29
  10.5 40.1 %all_to_all.10 = bf16[64,16,128]{2,1,0:T(8,128)(2,1)S(1)} all-to-all(bf16[64,16,128]{2,1,0:T(8,128)(2,1)S(1)} %pad_maximum_fusion.2), channel_id=1, replica_groups=mesh['seq'=64,'chan'=8] {'seq'}, dimensions={0} | all-to-all | bytes 524288 | tf_op jit(solution)/shard_map/all_to_all | solution.py:40
  50.6 1.4 fusion.8
  52.0 0.0 copy-start
  52.0 1.0 multiply_add_fusion
  53.0 0.0 copy-start.2
  53.0 0.0 copy-start.3
  53.0 0.1 pad_maximum_fusion
  53.1 0.0 copy-done.1
  53.1 0.0 copy-start.5
  53.1 0.0 copy-start.4
  53.1 0.0 copy-start.6
  53.1 1.5 fusion.1
  54.6 0.1 multiply_subtract_fusion.2
  54.7 0.0 copy-done
  54.7 0.6 fusion.3
  55.3 0.0 copy-done.2
  55.3 0.0 copy-done.3
  55.3 0.1 multiply_subtract_fusion.1
  55.4 0.0 copy-done.5
  55.4 0.5 fusion
  55.9 0.7 copy.33
  56.7 4.2 %all-to-all-start.1 = ((bf16[64,8,128]{2,1,0:T(8,128)(2,1)}), bf16[64,8,128]{2,1,0:T(8,128)(2,1)S(1)}, u32[]{:S(2)}, u32[]{:S(2)}) async-start(bf16[64,8,128]{2,1,0:T(8,128)(2,1)} %copy.33), calls=%async_computation.1 | async-start | bytes 262144 | tf_op jit(solution)/shard_map/all_to_all | solution.py:54
  60.8 0.0 all-gather.3.cloned.1.call-start
  60.9 0.0 copy-done.4
  60.9 0.1 copy.26
  61.0 16.8 %all-to-all-done.1 = bf16[64,8,128]{2,1,0:T(8,128)(2,1)S(1)} async-done(((bf16[64,8,128]{2,1,0:T(8,128)(2,1)}), bf16[64,8,128]{2,1,0:T(8,128)(2,1)S(1)}, u32[]{:S(2)}, u32[]{:S(2)}) %all-to-all-start.1) | async-done | bytes 131104 | tf_op jit(solution)/shard_map/all_to_all | solution.py:54
  77.8 0.0 copy-done.6
  77.8 0.8 multiply_convert_fusion
  78.6 0.0 all-gather.3.cloned.1.call-update
  78.6 0.0 all-gather.5.cloned.1.call-start
  78.7 0.7 all-gather.5.cloned.1.call-update
  79.4 0.8 copy.34
  80.3 50.2 %all-gather.3.cloned.1.call-done = bf16[128,4096]{0,1:T(8,128)(2,1)} async-done(((bf16[128,512]{0,1:T(8,128)(2,1)}), bf16[128,4096]{0,1:T(8,128)(2,1)}) %all-gather.3.cloned.1.call-update) | async-done | bytes 1048592 | tf_op jit(solution)/shard_map/all_gather | solution.py:58
  130.5 127.5 %all-gather.5.cloned.1.call-done = bf16[4096,512]{1,0:T(8,128)(2,1)} async-done(((bf16[64,512]{1,0:T(8,128)(2,1)}), bf16[4096,512]{1,0:T(8,128)(2,1)}) %all-gather.5.cloned.1.call-update) | async-done | bytes 4194320 | tf_op jit(solution)/shard_map/all_gather | solution.py:61
  257.9 3.9 %convolution_convert_fusion = bf16[128,512]{1,0:T(8,128)(2,1)} fusion(bf16[128,4096]{0,1:T(8,128)(2,1)} %all-gather.3.cloned.1.call-done, bf16[4096,512]{1,0:T(8,128)(2,1)} %all-gather.5.cloned.1.call-done), kind=kOutput, calls=%fused_computation | convolution fusion | flops 536936448 | bytes 5373952 | tf_op jit(solution)/shard_map/dot_general | solution.py:59
  (4 shorter events, 0.1 us)
Async XLA Ops:
  7.2 45.9 %copy-start.1 = (f32[256,256,1]{1,0,2:T(8,128)S(1)}, f32[256,256,1]{1,0,2:T(8,128)}, u32[]{:S(2)}) copy-start(f32[256,256,1]{1,0,2:T(8,128)} %constant.21) | copy-start | bytes 786436
  52.0 2.7 %copy-start = (f32[256,256,1]{1,0,2:T(8,128)S(1)}, f32[256,256,1]{1,0,2:T(8,128)}, u32[]{:S(2)}) copy-start(f32[256,256,1]{1,0,2:T(8,128)} %constant.22) | copy-start | bytes 786436
  53.0 2.3 copy-start.2
  53.0 2.3 copy-start.3
  53.1 2.3 copy-start.5
  53.1 7.8 %copy-start.4 = (bf16[128,512]{1,0:T(8,128)(2,1)S(1)}, bf16[128,512]{1,0:T(8,128)(2,1)}, u32[]{:S(2)}) copy-start(bf16[128,512]{1,0:T(8,128)(2,1)} %param.12) | copy-start | bytes 393220
  53.1 24.7 %copy-start.6 = (f32[512]{0:T(512)S(1)}, f32[512]{0:T(512)}, u32[]{:S(2)}) copy-start(f32[512]{0:T(512)} %param.16) | copy-start | bytes 6148
  56.7 21.2 %all-to-all-start.1 = ((bf16[64,8,128]{2,1,0:T(8,128)(2,1)}), bf16[64,8,128]{2,1,0:T(8,128)(2,1)S(1)}, u32[]{:S(2)}, u32[]{:S(2)}) async-start(bf16[64,8,128]{2,1,0:T(8,128)(2,1)} %copy.33), calls=%async_computation.1 | async-start | bytes 262144 | tf_op jit(solution)/shard_map/all_to_all | solution.py:54
  60.8 69.6 %all-gather.3.cloned.1.call-start = ((), (), s32[]{:S(2)}) async-start(), calls=%async_computation.2 | async-start | bytes 1179648 | tf_op jit(solution)/shard_map/all_gather | solution.py:58
  78.6 179.3 %all-gather.5.cloned.1.call-start = ((), (), s32[]{:S(2)}) async-start(), calls=%async_computation.3 | async-start | bytes 4259840 | tf_op jit(solution)/shard_map/all_gather | solution.py:61
Sparse Core Ops, SparseCore 0:
  78.8 51.6 all-gather.2
  132.6 125.2 all-gather.4

commit v2 on v1

v2 whole, which is shorter than its diff:
```python
import functools
import math

import jax
import jax.numpy as jnp
import ml_dtypes
import numpy as np
from jax import lax
from jax.experimental import pallas as pl
from jax.experimental.pallas import tpu as pltpu
from jax.sharding import PartitionSpec as P

MESH = pl.DeviceIdType.MESH
BF16 = jnp.bfloat16
F32 = jnp.float32

SEQ = 64
ZLEN = 16
CHAN = 8
ROWS = 128
SLAB = 512
OWN = 8
WROWS = 64


def split(a):
    hi = a.astype(ml_dtypes.bfloat16)
    lo = (a - hi.astype(np.float64)).astype(ml_dtypes.bfloat16)
    return hi, lo


def tables():
    length = 2 * SEQ * ROWS
    half = np.arange(SEQ) + 0.5
    angle = 2.0 * math.pi / (2 * SEQ) * np.outer(half, np.arange(SEQ))
    first = np.concatenate([np.cos(angle), -np.sin(angle)], axis=0)
    last = first.T * (2.0 / length)
    twist = 2.0 * math.pi / length * np.outer(half, np.arange(ROWS))
    second = 2.0 * math.pi / ROWS * (np.outer(np.arange(ROWS), np.arange(ROWS)) % ROWS)
    c, s = np.cos(second), np.sin(second)
    forward = np.block([[c, -s], [s, c]])
    backward = np.block([[c, s], [-s, c]])
    f_hi, f_lo = split(first)
    l_hi, l_lo = split(last)
    w_hi, w_lo = split(forward)
    b_hi, b_lo = split(backward)
    return (
        np.concatenate([f_hi, f_lo], axis=1),
        np.stack([w_hi, w_lo, b_hi, b_lo]),
        np.concatenate([l_hi, l_lo, l_hi], axis=1),
        np.stack([np.cos(twist), np.sin(twist)]).astype(np.float32),
    )


def dot(a, b):
    return jnp.dot(a, b, preferred_element_type=F32)


def halves(a):
    hi = a.astype(BF16)
    return hi, (a - hi.astype(F32)).astype(BF16)


def kernel(
    q_ref, k_ref, v_ref, t_ref, skip_ref, w_ref, first_ref, second_ref, last_ref, twist_ref,
    out_ref, conv_ref,
    send_in, recv_in, send_back, recv_back, wide, freq, spread_hi, spread_lo, back_f, gated, weight,
    in_s, in_r, back_s, back_r, local, up_s, up_r, down_s, down_r, x_s, x_r, core_s, core_r, core2_s, core2_r,
    ga_s, ga_r,
):
    me = lax.axis_index("seq")
    slab = lax.axis_index("chan")
    x_lo, z, core = me // 32, (me % 32) // 2, me % 2
    y, x_hi = slab // 2, slab % 2
    ring = x_lo * 2 + core
    up = x_lo * 32 + ((z + 1) % ZLEN) * 2 + core
    down = x_lo * 32 + ((z + ZLEN - 1) % ZLEN) * 2 + core
    across = (1 - x_lo) * 32 + z * 2 + core
    twin = x_lo * 32 + z * 2 + (1 - core)

    def remote(src, dst, ss, rs, **where):
        return pltpu.make_async_remote_copy(
            src_ref=src, dst_ref=dst, send_sem=ss, recv_sem=rs, device_id=where, device_id_type=MESH
        )

    barrier = pltpu.get_barrier_semaphore()

    def greet(off, carry):
        pl.semaphore_signal(barrier, inc=1, device_id={"seq": (me + off) % SEQ}, device_id_type=MESH)
        return carry

    lax.fori_loop(1, SEQ, greet, 0)
    column = [((y + dy) % 4) * 2 + x_hi for dy in (1, 3, 2)]
    beside = y * 2 + (1 - x_hi)
    for other in column + [beside]:
        pl.semaphore_signal(barrier, inc=1, device_id={"chan": other}, device_id_type=MESH)

    signal = k_ref[...].astype(F32) * v_ref[...].astype(F32)
    send_in[...] = jnp.concatenate(
        [signal.T.reshape(SEQ, OWN, ROWS), t_ref[...].T.reshape(SEQ, OWN, ROWS)], axis=1
    ).astype(BF16)
    weight[ring, 0] = w_ref[...]

    pl.semaphore_wait(barrier, SEQ - 1 + 4)

    def exchange(source, target, ss, rs):
        def some(i, carry):
            step = 8 - (i + 1) // 2
            dz = jnp.where(i % 2 == 0, step, ZLEN - step) % ZLEN
            for dx in (0, 1):
                for dc in (0, 1):
                    there = ((x_lo + dx) % 2) * 32 + ((z + dz) % ZLEN) * 2 + (core + dc) % 2
                    remote(source.at[there], target.at[me], ss, rs, seq=there).start()
            return carry

        lax.fori_loop(0, 15, some, 0)
        for dx, dc in ((1, 0), (1, 1), (0, 1)):
            there = ((x_lo + dx) % 2) * 32 + z * 2 + (core + dc) % 2
            remote(source.at[there], target.at[me], ss, rs, seq=there).start()
        own = pltpu.make_async_copy(source.at[me], target.at[me], local)
        own.start()
        own.wait()

    def drain(buffer, sem):
        view = buffer.at[pl.ds(0, SEQ - 1)]
        pltpu.make_async_copy(view, view, sem).wait()

    def up_copy(t):
        return remote(weight.at[ring, (ZLEN - t) % ZLEN], weight.at[ring, 15 - t], up_s.at[t], up_r.at[t], seq=up)

    def down_copy(t):
        return remote(weight.at[ring, t], weight.at[ring, t + 1], down_s.at[t], down_r.at[t], seq=down)

    other_ring = (1 - x_lo) * 2 + core

    def part(r, i):
        return weight.at[r, pl.ds(4 * i, 4)]

    def x_copy(i):
        return remote(part(ring, i), part(ring, i), x_s.at[i], x_r.at[i], seq=across)

    def core_copy(i):
        return remote(part(ring, i), part(ring, i), core_s.at[i], core_r.at[i], seq=twin)

    def core2_copy(i):
        return remote(part(other_ring, i), part(other_ring, i), core2_s.at[i], core2_r.at[i], seq=twin)

    def ring_step(t):
        up_copy(t).wait_recv()
        if t < 7:
            up_copy(t + 1).start()
            down_copy(t).wait_recv()
            if t < 6:
                down_copy(t + 1).start()
        done = {2: 0, 3: 3, 6: 1, 7: 2}.get(t)
        if done is not None:
            x_copy(done).start()
            core_copy(done).start()

    def pass_on(i):
        x_copy(i).wait_recv()
        core2_copy(i).start()

    exchange(send_in, recv_in, in_s, in_r)
    up_copy(0).start()
    down_copy(0).start()
    for t in range(4):
        ring_step(t)
    drain(recv_in, in_r)

    wide[...] = recv_in[...].astype(F32).reshape(SEQ * 16, ROWS)
    stacked = jnp.concatenate([wide[pl.ds(c, SEQ, stride=16), :] for c in range(16)], axis=1).astype(BF16)
    freq[...] = dot(first_ref[...], jnp.concatenate([stacked, stacked], axis=0))
    cos, sin = twist_ref[0], twist_ref[1]
    for c in range(16):
        cols = pl.ds(c * ROWS, ROWS)
        rows = pl.ds(c * SEQ, SEQ)
        re, im = freq[0:SEQ, cols], freq[SEQ : 2 * SEQ, cols]
        turned = jnp.concatenate([re * cos + im * sin, im * cos - re * sin], axis=1)
        spread_hi[rows, :], spread_lo[rows, :] = halves(turned)
    ring_step(4)
    hi, lo = spread_hi[...], spread_lo[...]
    spec = dot(hi, second_ref[0]) + dot(lo, second_ref[0]) + dot(hi, second_ref[1])
    n = OWN * SEQ
    sr, si, hr, hi_ = spec[:n, :ROWS], spec[:n, ROWS:], spec[n:, :ROWS], spec[n:, ROWS:]
    prod = jnp.concatenate([sr * hr - si * hi_, sr * hi_ + si * hr], axis=1)
    hi, lo = halves(prod)
    back = dot(hi, second_ref[2]) + dot(lo, second_ref[2]) + dot(hi, second_ref[3])
    ring_step(5)
    pieces_hi, pieces_lo = [], []
    for c in range(OWN):
        re, im = back[c * SEQ : (c + 1) * SEQ, :ROWS], back[c * SEQ : (c + 1) * SEQ, ROWS:]
        unturned = jnp.concatenate([re * cos - im * sin, im * cos + re * sin], axis=0)
        hi, lo = halves(unturned)
        pieces_hi.append(hi)
        pieces_lo.append(lo)
    u_hi, u_lo = jnp.concatenate(pieces_hi, axis=1), jnp.concatenate(pieces_lo, axis=1)
    done = dot(last_ref[...], jnp.concatenate([u_hi, u_hi, u_lo], axis=0))
    for c in range(OWN):
        back_f[pl.ds(c, SEQ, stride=OWN), :] = done[:, c * ROWS : (c + 1) * ROWS]
    send_back[...] = back_f[...].reshape(SEQ, OWN, ROWS).astype(BF16)

    exchange(send_back, recv_back, back_s, back_r)
    ring_step(6)
    ring_step(7)
    pass_on(0)
    pass_on(3)
    drain(recv_back, back_r)

    convolved = recv_back[...].astype(F32).reshape(SLAB, ROWS).T
    conv_ref[...] = convolved
    signal = k_ref[...].astype(F32) * v_ref[...].astype(F32)
    gated[slab] = (q_ref[...].astype(F32) * (convolved + skip_ref[...] * signal)).astype(BF16)

    def g_copy(source, i, other):
        return remote(gated.at[source], gated.at[source], ga_s.at[i], ga_r.at[i], chan=other)

    sends = [g_copy(slab, 3, beside)] + [g_copy(slab, i, column[i]) for i in range(3)]
    for copy in sends:
        copy.start()
    g_copy(beside, 3, beside).wait_recv()
    more = [g_copy(beside, 4 + i, column[i]) for i in range(3)]
    for copy in more:
        copy.start()
    pass_on(1)
    pass_on(2)
    for i in range(4):
        core_copy(i).wait_recv()
        core2_copy(i).wait_recv()

    def term(source):
        blocks = []
        for j in range(4):
            rel = (4 * (source % 4) + j + ZLEN - z) % ZLEN
            for half in (0, 1):
                blocks.append(weight[(source // 4) * 2 + half, rel])
        return dot(gated[source], jnp.concatenate(blocks, axis=0))

    total = term(slab) + term(beside)
    for base, flip in ((0, False), (4, True)):
        for i, dy in enumerate((3, 1, 2)):
            source = ((y + dy) % 4) * 2 + (1 - x_hi if flip else x_hi)
            g_copy(source, base + i, column[i]).wait_recv()
            total = total + term(source)
    out_ref[...] = total.astype(BF16)

    drain(send_in, in_s)
    drain(send_back, back_s)
    for t in range(8):
        up_copy(t).wait_send()
        if t < 7:
            down_copy(t).wait_send()
    for i in range(4):
        x_copy(i).wait_send()
        core_copy(i).wait_send()
        core2_copy(i).wait_send()
    for copy in sends + more:
        copy.wait_send()


def body(query_proj, key_proj, value_proj, filter_taps, skip_bias, out_weight):
    dma = pltpu.SemaphoreType.DMA
    vmem = pl.BlockSpec(memory_space=pltpu.VMEM)
    consts = [jnp.asarray(t) for t in tables()]
    return pl.pallas_call(
        kernel,
        out_shape=(
            jax.ShapeDtypeStruct((ROWS, SLAB), BF16),
            jax.ShapeDtypeStruct((ROWS, SLAB), F32),
        ),
        in_specs=[vmem] * 10,
        out_specs=(vmem, vmem),
        scratch_shapes=[
            pltpu.VMEM((SEQ, 16, ROWS), BF16),
            pltpu.VMEM((SEQ, 16, ROWS), BF16),
            pltpu.VMEM((SEQ, OWN, ROWS), BF16),
            pltpu.VMEM((SEQ, OWN, ROWS), BF16),
            pltpu.VMEM((SEQ * 16, ROWS), F32),
            pltpu.VMEM((2 * SEQ, 16 * ROWS), F32),
            pltpu.VMEM((16 * SEQ, 2 * ROWS), BF16),
            pltpu.VMEM((16 * SEQ, 2 * ROWS), BF16),
            pltpu.VMEM((SEQ * OWN, ROWS), F32),
            pltpu.VMEM((CHAN, ROWS, SLAB), BF16),
            pltpu.VMEM((4, ZLEN, WROWS, SLAB), BF16),
            dma, dma, dma, dma, dma,
            dma((8,)), dma((8,)), dma((7,)), dma((7,)),
            dma((4,)), dma((4,)), dma((4,)), dma((4,)), dma((4,)), dma((4,)),
            dma((7,)), dma((7,)),
        ],
        compiler_params=pltpu.CompilerParams(
            collective_id=0, has_side_effects=True, vmem_limit_bytes=48 * 1024 * 1024
        ),
        name="hyena",
    )(query_proj, key_proj, value_proj, filter_taps, skip_bias.reshape(1, SLAB), out_weight, *consts)


def solution(mesh):
    return jax.shard_map(
        body,
        mesh=mesh,
        in_specs=(
            P("seq", "chan"),
            P("seq", "chan"),
            P("seq", "chan"),
            P("seq", "chan"),
            P("chan"),
            P("seq", "chan"),
        ),
        out_specs=(P("seq", "chan"), P("seq", "chan")),
        check_vma=False,
    )
```

time: 269 us -> 87.1 us (0.32)
  waiting for transfers between devices: 195 us -> 0 us
  Pallas kernels: 0 us -> 75 us
  blocking collectives: 40.1 us -> 0 us
  between operations: 14.3 us -> 0.66 us
  matrix products: 7.83 us -> 0 us
  local copies, waits for them, and re-layouts: 4.91 us -> 9.97 us
  starting transfers between devices: 4.27 us -> 0 us
    all_gather x2 -> x0, waiting for transfers between devices: 178 us -> none  [the longest x1 127 us: body(): lax.all_gather(out_weight, 'seq', axis=0, tiled=True)]
    pallas_call x0 -> x1, Pallas kernels: none -> 75 us  [body(): pl.pallas_call(kernel, out_shape=(jax.ShapeDtypeStruct((ROWS, SLAB), BF16...]
    all_to_all x1 -> x0, blocking collectives: 40.1 us -> none  [body(): lax.all_to_all(outgoing, 'seq', split_axis=0, concat_axis=0, tiled=True)]
    all_to_all x1 -> x0, waiting for transfers between devices: 16.8 us -> none  [body(): lax.all_to_all(conv.astype(jnp.bfloat16), 'seq', split_axis=0, concat_axi...]
    dot_general x5 -> x0, matrix products: 7.83 us -> none  [the longest x1 3.92 us: body(): jnp.dot(whole, lax.all_gather(out_weight, 'seq', axis=0, tiled=True), pre...]
    unnamed x19 -> x22, local copies, waits for them, and re-layouts: 4.16 us -> 9.97 us
    all_to_all x1 -> x0, starting transfers between devices: 4.19 us -> none  [body(): lax.all_to_all(conv.astype(jnp.bfloat16), 'seq', split_axis=0, concat_axi...]
  transfers between devices with their start and end apart: 3 -> 0, of which waited for: 3 -> 0; matrix products, arithmetic and copies ran while one was open for 0% -> 0% of each run, Pallas kernels for 0% -> 0%
where the time goes in v2:
time: 87.1 us; the launch traced here: 85.6 us
  Pallas kernels  75 us (86%)
  local copies, waits for them, and re-layouts  9.97 us (11%)
    pallas_call x1, Pallas kernels, body(): pl.pallas_call(kernel, out_shape=(jax.ShapeDtypeStruct((ROWS, SLAB), BF16...  75 us
    unnamed x22, local copies, waits for them, and re-layouts  9.97 us

profile of v2, /device:TPU:1, one launch (start us, length us, event | category | flops | bytes accessed | tf_op | source)
XLA Modules:
  0.0 85.6 jit_solution(7489484506874829709)
XLA Ops:
  0.6 0.0 copy-start
  0.6 1.0 %copy-done = bf16[4,256,256]{2,1,0:T(8,128)(2,1)S(1)} copy-done((bf16[4,256,256]{2,1,0:T(8,128)(2,1)S(1)}, bf16[4,256,256]{2,1,0:T(8,128)(2,1)}, u32[]{:S(2)}) %copy-start) | copy-done | bytes 524312
  1.7 0.0 copy-start.1
  1.7 0.9 %copy-done.1 = f32[128,512]{1,0:T(8,128)S(1)} copy-done((f32[128,512]{1,0:T(8,128)S(1)}, f32[128,512]{1,0:T(8,128)}, u32[]{:S(2)}) %copy-start.1) | copy-done | bytes 262168
  2.6 0.0 copy-start.2
  2.6 0.9 %copy-done.2 = bf16[128,512]{1,0:T(8,128)(2,1)S(1)} copy-done((bf16[128,512]{1,0:T(8,128)(2,1)S(1)}, bf16[128,512]{1,0:T(8,128)(2,1)}, u32[]{:S(2)}) %copy-start.2) | copy-done | bytes 131096
  3.5 0.0 copy-start.3
  3.5 0.9 %copy-done.3 = bf16[128,512]{1,0:T(8,128)(2,1)S(1)} copy-done((bf16[128,512]{1,0:T(8,128)(2,1)S(1)}, bf16[128,512]{1,0:T(8,128)(2,1)}, u32[]{:S(2)}) %copy-start.3) | copy-done | bytes 131096
  4.4 0.0 copy-start.4
  4.4 0.9 %copy-done.4 = bf16[128,512]{1,0:T(8,128)(2,1)S(1)} copy-done((bf16[128,512]{1,0:T(8,128)(2,1)S(1)}, bf16[128,512]{1,0:T(8,128)(2,1)}, u32[]{:S(2)}) %copy-start.4) | copy-done | bytes 131096
  5.3 0.0 copy-start.5
  5.3 0.8 copy-done.5
  6.2 0.0 copy-start.6
  6.2 0.8 copy-done.6
  7.0 0.0 copy-start.7
  7.0 0.8 copy-done.7
  7.8 0.0 copy-start.8
  7.8 0.8 copy-done.8
  8.6 0.0 copy-start.9
  8.6 0.7 copy-done.9
  9.3 75.0 %hyena.1 = (bf16[128,512]{1,0:T(8,128)(2,1)S(1)}, f32[128,512]{1,0:T(8,128)S(1)}) custom-call(bf16[128,512]{1,0:T(8,128)(2,1)S(1)} %copy-done.2, bf16[128,512]{1,0:T(8,128)(2,1)S(1)} %copy-done.3, bf16[128,512]{1,0:T(8,128)(2,1)S(1)} %copy-done.4, f32[128,512]{1,0:T(8,128)S(1)} %copy-done.1, f32[1,512]{1,0:T(1,128)S(1)} %bitcast.1, ...), custom_call_target="tpu_custom_call" | custom-call | tf_op jit(solution)/shard_map/hyena/pallas_call | solution.py:265
  84.2 0.7 copy.14
  84.9 0.7 copy.15
Async XLA Ops:
  0.6 1.0 %copy-start = (bf16[4,256,256]{2,1,0:T(8,128)(2,1)S(1)}, bf16[4,256,256]{2,1,0:T(8,128)(2,1)}, u32[]{:S(2)}) copy-start(bf16[4,256,256]{2,1,0:T(8,128)(2,1)} %constant.9.clone.second_ref) | copy-start | bytes 1572868
  1.7 0.9 %copy-start.1 = (f32[128,512]{1,0:T(8,128)S(1)}, f32[128,512]{1,0:T(8,128)}, u32[]{:S(2)}) copy-start(f32[128,512]{1,0:T(8,128)} %t_ref.1) | copy-start | bytes 786436
  2.6 0.9 %copy-start.2 = (bf16[128,512]{1,0:T(8,128)(2,1)S(1)}, bf16[128,512]{1,0:T(8,128)(2,1)}, u32[]{:S(2)}) copy-start(bf16[128,512]{1,0:T(8,128)(2,1)} %q_ref.1) | copy-start | bytes 393220
  3.5 0.9 %copy-start.3 = (bf16[128,512]{1,0:T(8,128)(2,1)S(1)}, bf16[128,512]{1,0:T(8,128)(2,1)}, u32[]{:S(2)}) copy-start(bf16[128,512]{1,0:T(8,128)(2,1)} %k_ref.1) | copy-start | bytes 393220
  4.4 0.9 %copy-start.4 = (bf16[128,512]{1,0:T(8,128)(2,1)S(1)}, bf16[128,512]{1,0:T(8,128)(2,1)}, u32[]{:S(2)}) copy-start(bf16[128,512]{1,0:T(8,128)(2,1)} %v_ref.1) | copy-start | bytes 393220
  5.3 0.8 copy-start.5
  6.2 0.8 copy-start.6
  7.0 0.8 copy-start.7
  7.8 0.8 copy-start.8
  8.6 0.7 copy-start.9

commit v3 on v2

--- a/solution.py
+++ b/solution.py
@@ -21,6 +21,7 @@
 SLAB = 512
 OWN = 8
 WROWS = 64
+PAIRS = (0, 14, 2, 12, 4, 10, 6, 8)
 
 
 def split(a):
@@ -42,13 +43,14 @@
     backward = np.block([[c, s], [-s, c]])
     f_hi, f_lo = split(first)
     l_hi, l_lo = split(last)
-    w_hi, w_lo = split(forward)
-    b_hi, b_lo = split(backward)
-    return (
-        np.concatenate([f_hi, f_lo], axis=1),
-        np.stack([w_hi, w_lo, b_hi, b_lo]),
-        np.concatenate([l_hi, l_lo, l_hi], axis=1),
-        np.stack([np.cos(twist), np.sin(twist)]).astype(np.float32),
+    return tuple(
+        table.astype(np.float32)
+        for table in (
+            np.concatenate([f_hi, f_lo], axis=1),
+            np.stack([forward, backward]),
+            np.concatenate([l_hi, l_lo, l_hi], axis=1),
+            np.stack([np.cos(twist), np.sin(twist)]),
+        )
     )
 
 
@@ -62,11 +64,13 @@
 
 
 def kernel(
-    q_ref, k_ref, v_ref, t_ref, skip_ref, w_ref, first_ref, second_ref, last_ref, twist_ref,
+    q_hbm, k_hbm, v_hbm, t_hbm, skip_hbm, w_hbm, first_hbm, second_hbm, last_hbm, twist_hbm,
     out_ref, conv_ref,
-    send_in, recv_in, send_back, recv_back, wide, freq, spread_hi, spread_lo, back_f, gated, weight,
-    in_s, in_r, back_s, back_r, local, up_s, up_r, down_s, down_r, x_s, x_r, core_s, core_r, core2_s, core2_r,
-    ga_s, ga_r,
+    q_ref, k_ref, v_ref, t_ref, skip_ref, w_ref, first_f, second_f, last_f, twist_ref,
+    first_ref, second_ref, last_ref,
+    send_t, recv_t, send_s, recv_s, send_back, recv_back, wide, freq, spread_hi, spread_lo, taps_spec, gated, weight,
+    int_s, int_r, ins_s, ins_r, back_s, back_r, local, up_s, up_r, down_s, down_r, x_s, x_r, core_s, core_r, core2_s, core2_r,
+    ga_s, ga_r, fetch_s,
 ):
     me = lax.axis_index("seq")
     slab = lax.axis_index("chan")
@@ -83,6 +87,18 @@
             src_ref=src, dst_ref=dst, send_sem=ss, recv_sem=rs, device_id=where, device_id_type=MESH
         )
 
+    fetches = [
+        pltpu.make_async_copy(src, dst, fetch_s.at[i])
+        for i, (src, dst) in enumerate(
+            [
+                (t_hbm, t_ref), (w_hbm, w_ref), (k_hbm, k_ref), (v_hbm, v_ref), (first_hbm, first_f),
+                (second_hbm, second_f), (last_hbm, last_f), (twist_hbm, twist_ref), (q_hbm, q_ref), (skip_hbm, skip_ref),
+            ]
+        )
+    ]
+    for fetch in fetches:
+        fetch.start()
+
     barrier = pltpu.get_barrier_semaphore()
 
     def greet(off, carry):
@@ -95,12 +111,10 @@
     for other in column + [beside]:
         pl.semaphore_signal(barrier, inc=1, device_id={"chan": other}, device_id_type=MESH)
 
-    signal = k_ref[...].astype(F32) * v_ref[...].astype(F32)
-    send_in[...] = jnp.concatenate(
-        [signal.T.reshape(SEQ, OWN, ROWS), t_ref[...].T.reshape(SEQ, OWN, ROWS)], axis=1
-    ).astype(BF16)
+    for fetch in fetches[:2]:
+        fetch.wait()
+    send_t[...] = t_ref[...].T.reshape(SEQ, OWN, ROWS).astype(BF16)
     weight[ring, 0] = w_ref[...]
-
     pl.semaphore_wait(barrier, SEQ - 1 + 4)
 
     def exchange(source, target, ss, rs):
@@ -134,7 +148,7 @@
     other_ring = (1 - x_lo) * 2 + core
 
     def part(r, i):
-        return weight.at[r, pl.ds(4 * i, 4)]
+        return weight.at[r, pl.ds(PAIRS[i], 2)]
 
     def x_copy(i):
         return remote(part(ring, i), part(ring, i), x_s.at[i], x_r.at[i], seq=across)
@@ -152,41 +166,56 @@
             down_copy(t).wait_recv()
             if t < 6:
                 down_copy(t + 1).start()
-        done = {2: 0, 3: 3, 6: 1, 7: 2}.get(t)
-        if done is not None:
-            x_copy(done).start()
-            core_copy(done).start()
+        x_copy(t).start()
+        core_copy(t).start()
 
     def pass_on(i):
         x_copy(i).wait_recv()
         core2_copy(i).start()
 
-    exchange(send_in, recv_in, in_s, in_r)
     up_copy(0).start()
     down_copy(0).start()
-    for t in range(4):
-        ring_step(t)
-    drain(recv_in, in_r)
-
-    wide[...] = recv_in[...].astype(F32).reshape(SEQ * 16, ROWS)
-    stacked = jnp.concatenate([wide[pl.ds(c, SEQ, stride=16), :] for c in range(16)], axis=1).astype(BF16)
-    freq[...] = dot(first_ref[...], jnp.concatenate([stacked, stacked], axis=0))
+    exchange(send_t, recv_t, int_s, int_r)
+    for fetch in fetches[2:4]:
+        fetch.wait()
+    signal = k_ref[...].astype(F32) * v_ref[...].astype(F32)
+    send_s[...] = signal.T.reshape(SEQ, OWN, ROWS).astype(BF16)
+    ring_step(0)
+    exchange(send_s, recv_s, ins_s, ins_r)
+    for fetch in fetches[4:]:
+        fetch.wait()
+    first_ref[...] = first_f[...].astype(BF16)
+    last_ref[...] = last_f[...].astype(BF16)
+    for i in range(2):
+        second_ref[2 * i], second_ref[2 * i + 1] = halves(second_f[i])
     cos, sin = twist_ref[0], twist_ref[1]
-    for c in range(16):
-        cols = pl.ds(c * ROWS, ROWS)
-        rows = pl.ds(c * SEQ, SEQ)
-        re, im = freq[0:SEQ, cols], freq[SEQ : 2 * SEQ, cols]
-        turned = jnp.concatenate([re * cos + im * sin, im * cos - re * sin], axis=1)
-        spread_hi[rows, :], spread_lo[rows, :] = halves(turned)
-    ring_step(4)
-    hi, lo = spread_hi[...], spread_lo[...]
-    spec = dot(hi, second_ref[0]) + dot(lo, second_ref[0]) + dot(hi, second_ref[1])
-    n = OWN * SEQ
-    sr, si, hr, hi_ = spec[:n, :ROWS], spec[:n, ROWS:], spec[n:, :ROWS], spec[n:, ROWS:]
+
+    def transform(arrived):
+        wide[...] = arrived[...].astype(F32).reshape(SEQ * OWN, ROWS)
+        stacked = jnp.concatenate([wide[pl.ds(c, SEQ, stride=OWN), :] for c in range(OWN)], axis=1).astype(BF16)
+        freq[...] = dot(first_ref[...], jnp.concatenate([stacked, stacked], axis=0))
+        for c in range(OWN):
+            cols = pl.ds(c * ROWS, ROWS)
+            rows = pl.ds(c * SEQ, SEQ)
+            re, im = freq[0:SEQ, cols], freq[SEQ : 2 * SEQ, cols]
+            turned = jnp.concatenate([re * cos + im * sin, im * cos - re * sin], axis=1)
+            spread_hi[rows, :], spread_lo[rows, :] = halves(turned)
+        hi, lo = spread_hi[...], spread_lo[...]
+        return dot(hi, second_ref[0]) + dot(lo, second_ref[0]) + dot(hi, second_ref[1])
+
+    drain(recv_t, int_r)
+    taps_spec[...] = transform(recv_t)
+    ring_step(1)
+    drain(recv_s, ins_r)
+    spec = transform(recv_s)
+    ring_step(2)
+    pass_on(0)
+    sr, si, hr, hi_ = spec[:, :ROWS], spec[:, ROWS:], taps_spec[:, :ROWS], taps_spec[:, ROWS:]
     prod = jnp.concatenate([sr * hr - si * hi_, sr * hi_ + si * hr], axis=1)
     hi, lo = halves(prod)
     back = dot(hi, second_ref[2]) + dot(lo, second_ref[2]) + dot(hi, second_ref[3])
-    ring_step(5)
+    ring_step(3)
+    pass_on(1)
     pieces_hi, pieces_lo = [], []
     for c in range(OWN):
         re, im = back[c * SEQ : (c + 1) * SEQ, :ROWS], back[c * SEQ : (c + 1) * SEQ, ROWS:]
@@ -197,20 +226,20 @@
     u_hi, u_lo = jnp.concatenate(pieces_hi, axis=1), jnp.concatenate(pieces_lo, axis=1)
     done = dot(last_ref[...], jnp.concatenate([u_hi, u_hi, u_lo], axis=0))
     for c in range(OWN):
-        back_f[pl.ds(c, SEQ, stride=OWN), :] = done[:, c * ROWS : (c + 1) * ROWS]
-    send_back[...] = back_f[...].reshape(SEQ, OWN, ROWS).astype(BF16)
+        wide[pl.ds(c, SEQ, stride=OWN), :] = done[:, c * ROWS : (c + 1) * ROWS]
+    send_back[...] = wide[...].reshape(SEQ, OWN, ROWS).astype(BF16)
 
     exchange(send_back, recv_back, back_s, back_r)
-    ring_step(6)
-    ring_step(7)
-    pass_on(0)
+    ring_step(4)
+    pass_on(2)
+    drain(recv_back, back_r)
+    ring_step(5)
     pass_on(3)
-    drain(recv_back, back_r)
 
     convolved = recv_back[...].astype(F32).reshape(SLAB, ROWS).T
     conv_ref[...] = convolved
     signal = k_ref[...].astype(F32) * v_ref[...].astype(F32)
-    gated[slab] = (q_ref[...].astype(F32) * (convolved + skip_ref[...] * signal)).astype(BF16)
+    gated[slab] = (q_ref[...].astype(F32) * (convolved + skip_ref[...][None, :] * signal)).astype(BF16)
 
     def g_copy(source, i, other):
         return remote(gated.at[source], gated.at[source], ga_s.at[i], ga_r.at[i], chan=other)
@@ -218,13 +247,16 @@
     sends = [g_copy(slab, 3, beside)] + [g_copy(slab, i, column[i]) for i in range(3)]
     for copy in sends:
         copy.start()
+    ring_step(6)
+    pass_on(4)
     g_copy(beside, 3, beside).wait_recv()
     more = [g_copy(beside, 4 + i, column[i]) for i in range(3)]
     for copy in more:
         copy.start()
-    pass_on(1)
-    pass_on(2)
-    for i in range(4):
+    ring_step(7)
+    for i in (5, 6, 7):
+        pass_on(i)
+    for i in range(8):
         core_copy(i).wait_recv()
         core2_copy(i).wait_recv()
 
@@ -244,13 +276,14 @@
             total = total + term(source)
     out_ref[...] = total.astype(BF16)
 
-    drain(send_in, in_s)
+    drain(send_t, int_s)
+    drain(send_s, ins_s)
     drain(send_back, back_s)
     for t in range(8):
         up_copy(t).wait_send()
         if t < 7:
             down_copy(t).wait_send()
-    for i in range(4):
+    for i in range(8):
         x_copy(i).wait_send()
         core_copy(i).wait_send()
         core2_copy(i).wait_send()
@@ -268,30 +301,45 @@
             jax.ShapeDtypeStruct((ROWS, SLAB), BF16),
             jax.ShapeDtypeStruct((ROWS, SLAB), F32),
         ),
-        in_specs=[vmem] * 10,
+        in_specs=[pl.BlockSpec(memory_space=pltpu.HBM)] * 10,
         out_specs=(vmem, vmem),
         scratch_shapes=[
-            pltpu.VMEM((SEQ, 16, ROWS), BF16),
-            pltpu.VMEM((SEQ, 16, ROWS), BF16),
-            pltpu.VMEM((SEQ, OWN, ROWS), BF16),
-            pltpu.VMEM((SEQ, OWN, ROWS), BF16),
-            pltpu.VMEM((SEQ * 16, ROWS), F32),
-            pltpu.VMEM((2 * SEQ, 16 * ROWS), F32),
-            pltpu.VMEM((16 * SEQ, 2 * ROWS), BF16),
-            pltpu.VMEM((16 * SEQ, 2 * ROWS), BF16),
+            pltpu.VMEM((ROWS, SLAB), BF16),
+            pltpu.VMEM((ROWS, SLAB), BF16),
+            pltpu.VMEM((ROWS, SLAB), BF16),
+            pltpu.VMEM((ROWS, SLAB), F32),
+            pltpu.VMEM((SLAB,), F32),
+            pltpu.VMEM((WROWS, SLAB), BF16),
+            pltpu.VMEM((2 * SEQ, 2 * SEQ), F32),
+            pltpu.VMEM((2, 2 * ROWS, 2 * ROWS), F32),
+            pltpu.VMEM((SEQ, 6 * SEQ), F32),
+            pltpu.VMEM((2, SEQ, ROWS), F32),
+            pltpu.VMEM((2 * SEQ, 2 * SEQ), BF16),
+            pltpu.VMEM((4, 2 * ROWS, 2 * ROWS), BF16),
+            pltpu.VMEM((SEQ, 6 * SEQ), BF16),
+            pltpu.VMEM((SEQ, OWN, ROWS), BF16),
+            pltpu.VMEM((SEQ, OWN, ROWS), BF16),
+            pltpu.VMEM((SEQ, OWN, ROWS), BF16),
+            pltpu.VMEM((SEQ, OWN, ROWS), BF16),
+            pltpu.VMEM((SEQ, OWN, ROWS), BF16),
+            pltpu.VMEM((SEQ, OWN, ROWS), BF16),
             pltpu.VMEM((SEQ * OWN, ROWS), F32),
+            pltpu.VMEM((2 * SEQ, OWN * ROWS), F32),
+            pltpu.VMEM((OWN * SEQ, 2 * ROWS), BF16),
+            pltpu.VMEM((OWN * SEQ, 2 * ROWS), BF16),
+            pltpu.VMEM((OWN * SEQ, 2 * ROWS), F32),
             pltpu.VMEM((CHAN, ROWS, SLAB), BF16),
             pltpu.VMEM((4, ZLEN, WROWS, SLAB), BF16),
-            dma, dma, dma, dma, dma,
+            dma, dma, dma, dma, dma, dma, dma,
             dma((8,)), dma((8,)), dma((7,)), dma((7,)),
-            dma((4,)), dma((4,)), dma((4,)), dma((4,)), dma((4,)), dma((4,)),
-            dma((7,)), dma((7,)),
+            dma((8,)), dma((8,)), dma((8,)), dma((8,)), dma((8,)), dma((8,)),
+            dma((7,)), dma((7,)), dma((10,)),
         ],
         compiler_params=pltpu.CompilerParams(
-            collective_id=0, has_side_effects=True, vmem_limit_bytes=48 * 1024 * 1024
+            collective_id=0, has_side_effects=True, vmem_limit_bytes=63 * 1024 * 1024
         ),
         name="hyena",
-    )(query_proj, key_proj, value_proj, filter_taps, skip_bias.reshape(1, SLAB), out_weight, *consts)
+    )(query_proj, key_proj, value_proj, filter_taps, skip_bias, out_weight, *consts)
 
 
 def solution(mesh):

time: 87.1 us -> 72 us (0.83); the launches traced: 85.6 us -> 71.6 us
  local copies, waits for them, and re-layouts: 9.97 us -> 2.32 us
  Pallas kernels: 75 us -> 68.6 us
    unnamed x22 -> x4, local copies, waits for them, and re-layouts: 9.97 us -> 2.32 us
    pallas_call x1, Pallas kernels: 75 us -> 68.6 us  [body(): pl.pallas_call(kernel, out_shape=(jax.ShapeDtypeStruct((ROWS, SLAB), BF16...]
where the time goes in v3:
time: 72 us; the launch traced here: 71.6 us
  Pallas kernels  68.6 us (95%)
  local copies, waits for them, and re-layouts  2.32 us (3%)
    pallas_call x1, Pallas kernels, body(): pl.pallas_call(kernel, out_shape=(jax.ShapeDtypeStruct((ROWS, SLAB), BF16...  68.6 us
    unnamed x4, local copies, waits for them, and re-layouts  2.32 us

profile of v3, /device:TPU:1, one launch (start us, length us, event | category | flops | bytes accessed | tf_op | source)
XLA Modules:
  0.0 71.6 jit_solution(2864210567297233676)
XLA Ops:
  0.6 68.6 %hyena.1 = (bf16[128,512]{1,0:T(8,128)(2,1)}, f32[128,512]{1,0:T(8,128)}) custom-call(bf16[128,512]{1,0:T(8,128)(2,1)} %q_hbm.1, bf16[128,512]{1,0:T(8,128)(2,1)} %k_hbm.1, bf16[128,512]{1,0:T(8,128)(2,1)} %v_hbm.1, f32[128,512]{1,0:T(8,128)} %t_hbm.1, f32[512]{0:T(512)} %skip_hbm.1, bf16[64,512]{1,0:T(8,128)(2,1)} %w_hbm.1, ...), custom_call_target="tpu_custom_call" | custom-call | tf_op jit(solution)/shard_map/hyena/pallas_call | solution.py:298
  69.3 0.0 copy-start
  69.3 1.6 %copy.14 = bf16[128,512]{1,0:T(8,128)(2,1)} copy(bf16[128,512]{1,0:T(8,128)(2,1)} %get-tuple-element.4) | data formatting | bytes 262144
  70.9 0.0 copy-done
  70.9 0.7 copy.15
Async XLA Ops:
  69.3 1.6 %copy-start = (f32[128,512]{1,0:T(8,128)S(1)}, f32[128,512]{1,0:T(8,128)}, u32[]{:S(2)}) copy-start(f32[128,512]{1,0:T(8,128)} %get-tuple-element.5) | copy-start | bytes 786436

commit v4 on v2

v4 whole, which is shorter than its diff:
```python
import functools
import math

import jax
import jax.numpy as jnp
import ml_dtypes
import numpy as np
from jax import lax
from jax.experimental import pallas as pl
from jax.experimental.pallas import tpu as pltpu
from jax.sharding import PartitionSpec as P

MESH = pl.DeviceIdType.MESH
BF16 = jnp.bfloat16
F32 = jnp.float32

SEQ = 64
ZLEN = 16
CHAN = 8
ROWS = 128
SLAB = 512
OWN = 8
WROWS = 64
PAIRS = (0, 14, 2, 12, 4, 10, 6, 8)


def split(a):
    hi = a.astype(ml_dtypes.bfloat16)
    lo = (a - hi.astype(np.float64)).astype(ml_dtypes.bfloat16)
    return hi, lo


def tables():
    length = 2 * SEQ * ROWS
    half = np.arange(SEQ) + 0.5
    angle = 2.0 * math.pi / (2 * SEQ) * np.outer(half, np.arange(SEQ))
    first = np.concatenate([np.cos(angle), -np.sin(angle)], axis=0)
    last = first.T * (2.0 / length)
    twist = 2.0 * math.pi / length * np.outer(half, np.arange(ROWS))
    second = 2.0 * math.pi / ROWS * (np.outer(np.arange(ROWS), np.arange(ROWS)) % ROWS)
    c, s = np.cos(second), np.sin(second)
    forward = np.block([[c, -s], [s, c]])
    backward = np.block([[c, s], [-s, c]])
    f_hi, f_lo = split(first)
    l_hi, l_lo = split(last)
    return tuple(
        table.astype(np.float32)
        for table in (
            np.concatenate([f_hi, f_lo], axis=1),
            np.stack([forward, backward]),
            np.concatenate([l_hi, l_lo, l_hi], axis=1),
            np.stack([np.cos(twist), np.sin(twist)]),
        )
    )


def dot(a, b):
    return jnp.dot(a, b, preferred_element_type=F32)


def halves(a):
    hi = a.astype(BF16)
    return hi, (a - hi.astype(F32)).astype(BF16)


def kernel(
    q_hbm, k_hbm, v_hbm, t_hbm, skip_hbm, w_hbm, first_hbm, second_hbm, last_hbm, twist_hbm,
    out_ref, conv_ref,
    q_ref, k_ref, v_ref, t_ref, skip_ref, w_ref, first_f, second_f, last_f, twist_ref,
    first_ref, second_ref, last_ref,
    send_in, recv_in, send_back, recv_back, wide, freq, spread_hi, spread_lo, back_f, gated, weight,
    in_s, in_r, back_s, back_r, up_s, up_r, down_s, down_r, x_s, x_r, core_s, core_r, core2_s, core2_r,
    far_s, far_r,
    ga_s, ga_r, fetch_s,
):
    me = lax.axis_index("seq")
    slab = lax.axis_index("chan")
    x_lo, z, core = me // 32, (me % 32) // 2, me % 2
    y, x_hi = slab // 2, slab % 2
    ring = x_lo * 2 + core
    up = x_lo * 32 + ((z + 1) % ZLEN) * 2 + core
    down = x_lo * 32 + ((z + ZLEN - 1) % ZLEN) * 2 + core
    across = (1 - x_lo) * 32 + z * 2 + core
    twin = x_lo * 32 + z * 2 + (1 - core)

    peers = []
    for dz in (8, 9, 7, 10, 6, 11, 5, 12, 4, 13, 3, 14, 2, 15, 1, 0):
        for dx, dc in ((1, 0), (1, 1), (0, 0), (0, 1)):
            if (dz, dx, dc) != (0, 0, 0):
                peers.append(((x_lo + dx) % 2) * 32 + ((z + dz) % ZLEN) * 2 + (core + dc) % 2)

    def remote(src, dst, ss, rs, **where):
        return pltpu.make_async_remote_copy(
            src_ref=src, dst_ref=dst, send_sem=ss, recv_sem=rs, device_id=where, device_id_type=MESH
        )

    fetches = [
        pltpu.make_async_copy(src, dst, fetch_s.at[i])
        for i, (src, dst) in enumerate(
            [
                (k_hbm, k_ref), (v_hbm, v_ref), (t_hbm, t_ref), (w_hbm, w_ref), (first_hbm, first_f),
                (second_hbm, second_f), (last_hbm, last_f), (twist_hbm, twist_ref), (q_hbm, q_ref), (skip_hbm, skip_ref),
            ]
        )
    ]
    for fetch in fetches:
        fetch.start()

    barrier = pltpu.get_barrier_semaphore()

    for there in peers:
        pl.semaphore_signal(barrier, inc=1, device_id={"seq": there}, device_id_type=MESH)
    column = [((y + dy) % 4) * 2 + x_hi for dy in (1, 3, 2)]
    beside = y * 2 + (1 - x_hi)
    for other in column + [beside]:
        pl.semaphore_signal(barrier, inc=1, device_id={"chan": other}, device_id_type=MESH)

    for fetch in fetches[:3]:
        fetch.wait()
    signal = k_ref[...].astype(F32) * v_ref[...].astype(F32)
    send_in[...] = jnp.concatenate(
        [signal.T.reshape(SEQ, OWN, ROWS), t_ref[...].T.reshape(SEQ, OWN, ROWS)], axis=1
    ).astype(BF16)
    fetches[3].wait()
    weight[ring, 0] = w_ref[...]
    pl.semaphore_wait(barrier, SEQ - 1 + 4)

    def exchange(source, target, ss, rs, part):
        for there in part:
            remote(source.at[there], target.at[me], ss, rs, seq=there).start()

    def drain(buffer, sem):
        view = buffer.at[pl.ds(0, SEQ - 1)]
        pltpu.make_async_copy(view, view, sem).wait()

    def up_copy(t):
        return remote(weight.at[ring, (ZLEN - t) % ZLEN], weight.at[ring, 15 - t], up_s.at[t], up_r.at[t], seq=up)

    def down_copy(t):
        return remote(weight.at[ring, t], weight.at[ring, t + 1], down_s.at[t], down_r.at[t], seq=down)

    other_ring = (1 - x_lo) * 2 + core

    def part(r, i, count=2):
        return weight.at[r, pl.ds(PAIRS[i], count)]

    def x_copy(i):
        count = 2 if i < 6 else 1
        return remote(part(ring, i, count), part(ring, i, count), x_s.at[i], x_r.at[i], seq=across)

    def core_copy(i):
        return remote(part(ring, i), part(ring, i), core_s.at[i], core_r.at[i], seq=twin)

    def core2_copy(i):
        return remote(part(other_ring, i), part(other_ring, i), core2_s.at[i], core2_r.at[i], seq=twin)

    def far_copy(i):
        src, dst, there = ((10, 9, up), (6, 7, down), (9, 8, up))[i]
        return remote(weight.at[other_ring, src], weight.at[other_ring, dst], far_s.at[i], far_r.at[i], seq=there)

    def ring_step(t):
        up_copy(t).wait_recv()
        if t < 7:
            up_copy(t + 1).start()
            down_copy(t).wait_recv()
            if t < 6:
                down_copy(t + 1).start()
        if t < 6:
            x_copy(t).start()
        if t == 5:
            x_copy(6).start()
        core_copy(t).start()

    def pass_on(i):
        if i < 6:
            x_copy(i).wait_recv()
        if i == 5:
            far_copy(0).start()
            x_copy(6).wait_recv()
            far_copy(1).start()
        if i == 6:
            far_copy(0).wait_recv()
            far_copy(2).start()
            far_copy(1).wait_recv()
        if i == 7:
            far_copy(2).wait_recv()
        core2_copy(i).start()

    up_copy(0).start()
    down_copy(0).start()
    exchange(send_in, recv_in, in_s, in_r, peers[:16])
    ring_step(0)
    exchange(send_in, recv_in, in_s, in_r, peers[16:32])
    ring_step(1)
    exchange(send_in, recv_in, in_s, in_r, peers[32:48])
    pass_on(0)
    exchange(send_in, recv_in, in_s, in_r, peers[48:])
    recv_in[me] = send_in[me]
    for fetch in fetches[4:]:
        fetch.wait()
    first_ref[...] = first_f[...].astype(BF16)
    last_ref[...] = last_f[...].astype(BF16)
    for i in range(2):
        second_ref[2 * i], second_ref[2 * i + 1] = halves(second_f[i])
    cos, sin = twist_ref[0], twist_ref[1]

    ring_step(2)
    pass_on(1)
    drain(recv_in, in_r)
    wide[...] = recv_in[...].astype(F32).reshape(SEQ * 16, ROWS)
    stacked = jnp.concatenate([wide[pl.ds(c, SEQ, stride=16), :] for c in range(16)], axis=1).astype(BF16)
    freq[...] = dot(first_ref[...], jnp.concatenate([stacked, stacked], axis=0))
    for c in range(16):
        cols = pl.ds(c * ROWS, ROWS)
        rows = pl.ds(c * SEQ, SEQ)
        re, im = freq[0:SEQ, cols], freq[SEQ : 2 * SEQ, cols]
        turned = jnp.concatenate([re * cos + im * sin, im * cos - re * sin], axis=1)
        spread_hi[rows, :], spread_lo[rows, :] = halves(turned)
    ring_step(3)
    pass_on(2)
    hi, lo = spread_hi[...], spread_lo[...]
    spec = dot(hi, second_ref[0]) + dot(lo, second_ref[0]) + dot(hi, second_ref[1])
    n = OWN * SEQ
    sr, si, hr, hi_ = spec[:n, :ROWS], spec[:n, ROWS:], spec[n:, :ROWS], spec[n:, ROWS:]
    prod = jnp.concatenate([sr * hr - si * hi_, sr * hi_ + si * hr], axis=1)
    hi, lo = halves(prod)
    back = dot(hi, second_ref[2]) + dot(lo, second_ref[2]) + dot(hi, second_ref[3])
    ring_step(4)
    pass_on(3)
    pieces_hi, pieces_lo = [], []
    for c in range(OWN):
        re, im = back[c * SEQ : (c + 1) * SEQ, :ROWS], back[c * SEQ : (c + 1) * SEQ, ROWS:]
        unturned = jnp.concatenate([re * cos - im * sin, im * cos + re * sin], axis=0)
        hi, lo = halves(unturned)
        pieces_hi.append(hi)
        pieces_lo.append(lo)
    u_hi, u_lo = jnp.concatenate(pieces_hi, axis=1), jnp.concatenate(pieces_lo, axis=1)
    done = dot(last_ref[...], jnp.concatenate([u_hi, u_hi, u_lo], axis=0))
    for c in range(OWN):
        back_f[pl.ds(c, SEQ, stride=OWN), :] = done[:, c * ROWS : (c + 1) * ROWS]
    send_back[...] = back_f[...].reshape(SEQ, OWN, ROWS).astype(BF16)

    exchange(send_back, recv_back, back_s, back_r, peers[:16])
    exchange(send_back, recv_back, back_s, back_r, peers[16:32])
    exchange(send_back, recv_back, back_s, back_r, peers[32:])
    ring_step(5)
    pass_on(4)
    recv_back[me] = send_back[me]
    drain(recv_back, back_r)

    pass_on(5)
    ring_step(6)
    half_slab = SLAB // 2

    def g_copy(source, half, i, other):
        return remote(gated.at[source, half], gated.at[source, half], ga_s.at[i], ga_r.at[i], chan=other)

    sends = []

    def g_send(*what):
        copy = g_copy(*what)
        copy.start()
        sends.append(copy)

    for half in range(2):
        cols = pl.ds(half * half_slab, half_slab)
        devs = pl.ds(half * (SEQ // 2), SEQ // 2)
        convolved = recv_back[devs].astype(F32).reshape(half_slab, ROWS).T
        conv_ref[:, cols] = convolved
        signal = k_ref[:, cols].astype(F32) * v_ref[:, cols].astype(F32)
        mixed_sum = convolved + skip_ref[cols][None, :] * signal
        gated[slab, half] = (q_ref[:, cols].astype(F32) * mixed_sum).astype(BF16)
        if half == 0:
            g_send(slab, 0, 0, beside)
        else:
            for i in range(3):
                g_send(slab, 1, 7 + i, column[i])
            g_send(slab, 1, 10, beside)
            for i in range(3):
                g_send(slab, 0, 1 + i, column[i])
    back_y = [((y + 4 - dy) % 4) * 2 + x_hi for dy in (1, 3, 2)]
    beyond = [((y + 4 - dy) % 4) * 2 + (1 - x_hi) for dy in (1, 3, 2)]
    pass_on(6)
    g_copy(beside, 0, 0, beside).wait_recv()
    for i in range(3):
        g_send(beside, 0, 4 + i, column[i])
    for i in range(3):
        g_copy(back_y[i], 1, 7 + i, column[i]).wait_recv()
        g_send(back_y[i], 1, 11 + i, beside)
    ring_step(7)
    pass_on(7)
    for i in range(8):
        core_copy(i).wait_recv()
        core2_copy(i).wait_recv()

    def term(source, half):
        blocks = []
        for j in range(2):
            rel = (4 * (source % 4) + 2 * half + j + ZLEN - z) % ZLEN
            for c in (0, 1):
                blocks.append(weight[(source // 4) * 2 + c, rel])
        return dot(gated[source, half], jnp.concatenate(blocks, axis=0))

    total = term(slab, 0) + term(slab, 1) + term(beside, 0)
    for i in range(3):
        total = total + term(back_y[i], 1)
    for i in range(3):
        g_copy(back_y[i], 0, 1 + i, column[i]).wait_recv()
        total = total + term(back_y[i], 0)
    g_copy(beside, 1, 10, beside).wait_recv()
    total = total + term(beside, 1)
    for i in range(3):
        g_copy(beyond[i], 0, 4 + i, column[i]).wait_recv()
        total = total + term(beyond[i], 0)
        g_copy(beyond[i], 1, 11 + i, beside).wait_recv()
        total = total + term(beyond[i], 1)
    out_ref[...] = total.astype(BF16)

    drain(send_in, in_s)
    drain(send_back, back_s)
    for t in range(8):
        up_copy(t).wait_send()
        if t < 7:
            down_copy(t).wait_send()
    for i in range(3):
        far_copy(i).wait_send()
    for i in range(8):
        if i < 7:
            x_copy(i).wait_send()
        core_copy(i).wait_send()
        core2_copy(i).wait_send()
    for copy in sends:
        copy.wait_send()


def body(query_proj, key_proj, value_proj, filter_taps, skip_bias, out_weight):
    dma = pltpu.SemaphoreType.DMA
    vmem = pl.BlockSpec(memory_space=pltpu.VMEM)
    consts = [jnp.asarray(t) for t in tables()]
    return pl.pallas_call(
        kernel,
        out_shape=(
            jax.ShapeDtypeStruct((ROWS, SLAB), BF16),
            jax.ShapeDtypeStruct((ROWS, SLAB), F32),
        ),
        in_specs=[pl.BlockSpec(memory_space=pltpu.HBM)] * 10,
        out_specs=(vmem, vmem),
        scratch_shapes=[
            pltpu.VMEM((ROWS, SLAB), BF16),
            pltpu.VMEM((ROWS, SLAB), BF16),
            pltpu.VMEM((ROWS, SLAB), BF16),
            pltpu.VMEM((ROWS, SLAB), F32),
            pltpu.VMEM((SLAB,), F32),
            pltpu.VMEM((WROWS, SLAB), BF16),
            pltpu.VMEM((2 * SEQ, 2 * SEQ), F32),
            pltpu.VMEM((2, 2 * ROWS, 2 * ROWS), F32),
            pltpu.VMEM((SEQ, 6 * SEQ), F32),
            pltpu.VMEM((2, SEQ, ROWS), F32),
            pltpu.VMEM((2 * SEQ, 2 * SEQ), BF16),
            pltpu.VMEM((4, 2 * ROWS, 2 * ROWS), BF16),
            pltpu.VMEM((SEQ, 6 * SEQ), BF16),
            pltpu.VMEM((SEQ, 16, ROWS), BF16),
            pltpu.VMEM((SEQ, 16, ROWS), BF16),
            pltpu.VMEM((SEQ, OWN, ROWS), BF16),
            pltpu.VMEM((SEQ, OWN, ROWS), BF16),
            pltpu.VMEM((SEQ * 16, ROWS), F32),
            pltpu.VMEM((2 * SEQ, 16 * ROWS), F32),
            pltpu.VMEM((16 * SEQ, 2 * ROWS), BF16),
            pltpu.VMEM((16 * SEQ, 2 * ROWS), BF16),
            pltpu.VMEM((SEQ * OWN, ROWS), F32),
            pltpu.VMEM((CHAN, 2, ROWS, SLAB // 2), BF16),
            pltpu.VMEM((4, ZLEN, WROWS, SLAB), BF16),
            dma, dma, dma, dma,
            dma((8,)), dma((8,)), dma((7,)), dma((7,)),
            dma((7,)), dma((7,)), dma((8,)), dma((8,)), dma((8,)), dma((8,)),
            dma((3,)), dma((3,)),
            dma((14,)), dma((14,)), dma((10,)),
        ],
        compiler_params=pltpu.CompilerParams(
            collective_id=0, has_side_effects=True, vmem_limit_bytes=48 * 1024 * 1024
        ),
        name="hyena",
    )(*[pltpu.with_memory_space_constraint(a, pltpu.HBM) for a in (query_proj, key_proj, value_proj, filter_taps, skip_bias, out_weight, *consts)])


def solution(mesh):
    return jax.shard_map(
        body,
        mesh=mesh,
        in_specs=(
            P("seq", "chan"),
            P("seq", "chan"),
            P("seq", "chan"),
            P("seq", "chan"),
            P("chan"),
            P("seq", "chan"),
        ),
        out_specs=(P("seq", "chan"), P("seq", "chan")),
        check_vma=False,
    )
```

time: 87.1 us -> 66.3 us (0.76)
  Pallas kernels: 75 us -> 63.4 us
  local copies, waits for them, and re-layouts: 9.97 us -> 1.36 us
    pallas_call x1, Pallas kernels: 75 us -> 63.4 us  [body(): pl.pallas_call(kernel, out_shape=(jax.ShapeDtypeStruct((ROWS, SLAB), BF16...]
    unnamed x22 -> x2, local copies, waits for them, and re-layouts: 9.97 us -> 1.36 us
where the time goes in v4:
time: 66.3 us; the launch traced here: 65.4 us
  Pallas kernels  63.4 us (96%)
  local copies, waits for them, and re-layouts  1.36 us (2%)
    pallas_call x1, Pallas kernels, body(): pl.pallas_call(kernel, out_shape=(jax.ShapeDtypeStruct((ROWS, SLAB), BF16...  63.4 us
    unnamed x2, local copies, waits for them, and re-layouts  1.36 us

profile of v4, /device:TPU:1, one launch (start us, length us, event | category | flops | bytes accessed | tf_op | source)
XLA Modules:
  0.0 65.4 jit_solution(17245773726928673014)
XLA Ops:
  0.6 63.4 %hyena.1 = (bf16[128,512]{1,0:T(8,128)(2,1)S(1)}, f32[128,512]{1,0:T(8,128)S(1)}) custom-call(bf16[128,512]{1,0:T(8,128)(2,1)} %q_hbm.1, bf16[128,512]{1,0:T(8,128)(2,1)} %k_hbm.1, bf16[128,512]{1,0:T(8,128)(2,1)} %v_hbm.1, f32[128,512]{1,0:T(8,128)} %t_hbm.1, f32[512]{0:T(512)} %skip_hbm.1, bf16[64,512]{1,0:T(8,128)(2,1)} %w_hbm.1, ...), custom_call_target="tpu_custom_call" | custom-call | tf_op jit(solution)/shard_map/hyena/pallas_call | solution.py:340
  64.0 0.7 %copy.14 = bf16[128,512]{1,0:T(8,128)(2,1)} copy(bf16[128,512]{1,0:T(8,128)(2,1)S(1)} %get-tuple-element.4) | data formatting | bytes 262144
  64.7 0.7 %copy.15 = f32[128,512]{1,0:T(8,128)} copy(f32[128,512]{1,0:T(8,128)S(1)} %get-tuple-element.5) | data formatting | bytes 524288

commit v5 on v4

--- a/solution.py
+++ b/solution.py
@@ -21,6 +21,7 @@
 SLAB = 512
 OWN = 8
 WROWS = 64
+SUB = 4
 PAIRS = (0, 14, 2, 12, 4, 10, 6, 8)
 
 
@@ -133,11 +134,16 @@
         view = buffer.at[pl.ds(0, SEQ - 1)]
         pltpu.make_async_copy(view, view, sem).wait()
 
-    def up_copy(t):
-        return remote(weight.at[ring, (ZLEN - t) % ZLEN], weight.at[ring, 15 - t], up_s.at[t], up_r.at[t], seq=up)
-
-    def down_copy(t):
-        return remote(weight.at[ring, t], weight.at[ring, t + 1], down_s.at[t], down_r.at[t], seq=down)
+    def piece(r, slot, k):
+        return weight.at[r, slot, pl.ds(k * (WROWS // SUB), WROWS // SUB)]
+
+    def up_copy(t, k):
+        src, dst = piece(ring, (ZLEN - t) % ZLEN, k), piece(ring, 15 - t, k)
+        return remote(src, dst, up_s.at[t * SUB + k], up_r.at[t * SUB + k], seq=up)
+
+    def down_copy(t, k):
+        src, dst = piece(ring, t, k), piece(ring, t + 1, k)
+        return remote(src, dst, down_s.at[t * SUB + k], down_r.at[t * SUB + k], seq=down)
 
     other_ring = (1 - x_lo) * 2 + core
 
@@ -154,17 +160,19 @@
     def core2_copy(i):
         return remote(part(other_ring, i), part(other_ring, i), core2_s.at[i], core2_r.at[i], seq=twin)
 
-    def far_copy(i):
+    def far_copy(i, k):
         src, dst, there = ((10, 9, up), (6, 7, down), (9, 8, up))[i]
-        return remote(weight.at[other_ring, src], weight.at[other_ring, dst], far_s.at[i], far_r.at[i], seq=there)
+        n = i * SUB + k
+        return remote(piece(other_ring, src, k), piece(other_ring, dst, k), far_s.at[n], far_r.at[n], seq=there)
 
     def ring_step(t):
-        up_copy(t).wait_recv()
-        if t < 7:
-            up_copy(t + 1).start()
-            down_copy(t).wait_recv()
-            if t < 6:
-                down_copy(t + 1).start()
+        for k in range(SUB):
+            up_copy(t, k).wait_recv()
+            if t < 7:
+                up_copy(t + 1, k).start()
+                down_copy(t, k).wait_recv()
+                if t < 6:
+                    down_copy(t + 1, k).start()
         if t < 6:
             x_copy(t).start()
         if t == 5:
@@ -175,19 +183,25 @@
         if i < 6:
             x_copy(i).wait_recv()
         if i == 5:
-            far_copy(0).start()
+            for k in range(SUB):
+                far_copy(0, k).start()
             x_copy(6).wait_recv()
-            far_copy(1).start()
+            for k in range(SUB):
+                far_copy(1, k).start()
         if i == 6:
-            far_copy(0).wait_recv()
-            far_copy(2).start()
-            far_copy(1).wait_recv()
+            for k in range(SUB):
+                far_copy(0, k).wait_recv()
+                far_copy(2, k).start()
+            for k in range(SUB):
+                far_copy(1, k).wait_recv()
         if i == 7:
-            far_copy(2).wait_recv()
+            for k in range(SUB):
+                far_copy(2, k).wait_recv()
         core2_copy(i).start()
 
-    up_copy(0).start()
-    down_copy(0).start()
+    for k in range(SUB):
+        up_copy(0, k).start()
+        down_copy(0, k).start()
     exchange(send_in, recv_in, in_s, in_r, peers[:16])
     ring_step(0)
     exchange(send_in, recv_in, in_s, in_r, peers[16:32])
@@ -318,12 +332,13 @@
 
     drain(send_in, in_s)
     drain(send_back, back_s)
-    for t in range(8):
-        up_copy(t).wait_send()
-        if t < 7:
-            down_copy(t).wait_send()
-    for i in range(3):
-        far_copy(i).wait_send()
+    for k in range(SUB):
+        for t in range(8):
+            up_copy(t, k).wait_send()
+            if t < 7:
+                down_copy(t, k).wait_send()
+        for i in range(3):
+            far_copy(i, k).wait_send()
     for i in range(8):
         if i < 7:
             x_copy(i).wait_send()
@@ -371,9 +386,9 @@
             pltpu.VMEM((CHAN, 2, ROWS, SLAB // 2), BF16),
             pltpu.VMEM((4, ZLEN, WROWS, SLAB), BF16),
             dma, dma, dma, dma,
-            dma((8,)), dma((8,)), dma((7,)), dma((7,)),
+            dma((8 * SUB,)), dma((8 * SUB,)), dma((7 * SUB,)), dma((7 * SUB,)),
             dma((7,)), dma((7,)), dma((8,)), dma((8,)), dma((8,)), dma((8,)),
-            dma((3,)), dma((3,)),
+            dma((3 * SUB,)), dma((3 * SUB,)),
             dma((14,)), dma((14,)), dma((10,)),
         ],
         compiler_params=pltpu.CompilerParams(

time: 66.3 us -> 65.6 us (0.989)
  no operation moved by 1% of the time
where the time goes in v5:
time: 65.6 us; the launch traced here: 64.9 us
  Pallas kernels  62.9 us (96%)
  local copies, waits for them, and re-layouts  1.36 us (2%)
    pallas_call x1, Pallas kernels, body(): pl.pallas_call(kernel, out_shape=(jax.ShapeDtypeStruct((ROWS, SLAB), BF16...  62.9 us
    unnamed x2, local copies, waits for them, and re-layouts  1.36 us

profile of v5, /device:TPU:1, one launch (start us, length us, event | category | flops | bytes accessed | tf_op | source)
XLA Modules:
  0.0 64.9 jit_solution(5670147962840127735)
XLA Ops:
  0.6 62.9 %hyena.1 = (bf16[128,512]{1,0:T(8,128)(2,1)S(1)}, f32[128,512]{1,0:T(8,128)S(1)}) custom-call(bf16[128,512]{1,0:T(8,128)(2,1)} %q_hbm.1, bf16[128,512]{1,0:T(8,128)(2,1)} %k_hbm.1, bf16[128,512]{1,0:T(8,128)(2,1)} %v_hbm.1, f32[128,512]{1,0:T(8,128)} %t_hbm.1, f32[512]{0:T(512)} %skip_hbm.1, bf16[64,512]{1,0:T(8,128)(2,1)} %w_hbm.1, ...), custom_call_target="tpu_custom_call" | custom-call | tf_op jit(solution)/shard_map/hyena/pallas_call | solution.py:355
  63.6 0.7 %copy.14 = bf16[128,512]{1,0:T(8,128)(2,1)} copy(bf16[128,512]{1,0:T(8,128)(2,1)S(1)} %get-tuple-element.4) | data formatting | bytes 262144
  64.2 0.7 %copy.15 = f32[128,512]{1,0:T(8,128)} copy(f32[128,512]{1,0:T(8,128)S(1)} %get-tuple-element.5) | data formatting | bytes 524288

commit v6 on v5

--- a/solution.py
+++ b/solution.py
@@ -215,7 +215,8 @@
     first_ref[...] = first_f[...].astype(BF16)
     last_ref[...] = last_f[...].astype(BF16)
     for i in range(2):
-        second_ref[2 * i], second_ref[2 * i + 1] = halves(second_f[i])
+        hi, lo = halves(second_f[i])
+        second_ref[i] = jnp.concatenate([hi, hi, lo], axis=0)
     cos, sin = twist_ref[0], twist_ref[1]
 
     ring_step(2)
@@ -233,12 +234,12 @@
     ring_step(3)
     pass_on(2)
     hi, lo = spread_hi[...], spread_lo[...]
-    spec = dot(hi, second_ref[0]) + dot(lo, second_ref[0]) + dot(hi, second_ref[1])
+    spec = dot(jnp.concatenate([hi, lo, hi], axis=1), second_ref[0])
     n = OWN * SEQ
     sr, si, hr, hi_ = spec[:n, :ROWS], spec[:n, ROWS:], spec[n:, :ROWS], spec[n:, ROWS:]
     prod = jnp.concatenate([sr * hr - si * hi_, sr * hi_ + si * hr], axis=1)
     hi, lo = halves(prod)
-    back = dot(hi, second_ref[2]) + dot(lo, second_ref[2]) + dot(hi, second_ref[3])
+    back = dot(jnp.concatenate([hi, lo, hi], axis=1), second_ref[1])
     ring_step(4)
     pass_on(3)
     pieces_hi, pieces_lo = [], []
@@ -372,7 +373,7 @@
             pltpu.VMEM((SEQ, 6 * SEQ), F32),
             pltpu.VMEM((2, SEQ, ROWS), F32),
             pltpu.VMEM((2 * SEQ, 2 * SEQ), BF16),
-            pltpu.VMEM((4, 2 * ROWS, 2 * ROWS), BF16),
+            pltpu.VMEM((2, 6 * ROWS, 2 * ROWS), BF16),
             pltpu.VMEM((SEQ, 6 * SEQ), BF16),
             pltpu.VMEM((SEQ, 16, ROWS), BF16),
             pltpu.VMEM((SEQ, 16, ROWS), BF16),

time: 65.6 us -> 65.6 us (level)
  no operation moved by 1% of the time
where the time goes in v6:
time: 65.6 us; the launch traced here: 64.9 us
  Pallas kernels  62.9 us (96%)
  local copies, waits for them, and re-layouts  1.36 us (2%)
    pallas_call x1, Pallas kernels, body(): pl.pallas_call(kernel, out_shape=(jax.ShapeDtypeStruct((ROWS, SLAB), BF16...  62.9 us
    unnamed x2, local copies, waits for them, and re-layouts  1.36 us

profile of v6, /device:TPU:1, one launch (start us, length us, event | category | flops | bytes accessed | tf_op | source)
XLA Modules:
  0.0 64.9 jit_solution(2408082854640478428)
XLA Ops:
  0.6 62.9 %hyena.1 = (bf16[128,512]{1,0:T(8,128)(2,1)S(1)}, f32[128,512]{1,0:T(8,128)S(1)}) custom-call(bf16[128,512]{1,0:T(8,128)(2,1)} %q_hbm.1, bf16[128,512]{1,0:T(8,128)(2,1)} %k_hbm.1, bf16[128,512]{1,0:T(8,128)(2,1)} %v_hbm.1, f32[128,512]{1,0:T(8,128)} %t_hbm.1, f32[512]{0:T(512)} %skip_hbm.1, bf16[64,512]{1,0:T(8,128)(2,1)} %w_hbm.1, ...), custom_call_target="tpu_custom_call" | custom-call | tf_op jit(solution)/shard_map/hyena/pallas_call | solution.py:356
  63.6 0.7 %copy.14 = bf16[128,512]{1,0:T(8,128)(2,1)} copy(bf16[128,512]{1,0:T(8,128)(2,1)S(1)} %get-tuple-element.4) | data formatting | bytes 262144
  64.2 0.7 %copy.15 = f32[128,512]{1,0:T(8,128)} copy(f32[128,512]{1,0:T(8,128)S(1)} %get-tuple-element.5) | data formatting | bytes 524288
